TPU v7x, 32 devices: a whole 2x2x4 slice. The times are simulated.
32 devices in a mesh: ctx: 4 (over x, core), fsdp: 4 (over z), batch: 2 (over y).
Axes of the slice: x: 2, y: 2, z: 4, core: 2. Of those that a mesh axis runs over, the one named last changes fastest.
Arguments:
- inputs: bfloat16 [2, 512, 4096], P('batch', 'ctx'), may hold values from -6 to 6
- values: bfloat16 [2, 512, 2048], P('batch', 'ctx', 'fsdp'), may hold values from -6 to 6
- w_qk: bfloat16 [4096, 256], P('fsdp'), may hold values from -0.09375 to 0.09375
- conv_qk: float32 [3, 256], P(None, 'fsdp'), may hold values from -3 to 3
- conv_v: float32 [3, 2048], P(None, 'fsdp'), may hold values from -3 to 3
- d_attn: bfloat16 [2, 512, 2048], P('batch', 'ctx', 'fsdp'), may hold values from -6 to 6
Outputs:
- attended: bfloat16 [2, 512, 2048], P('batch', 'ctx', 'fsdp')
- grad_v: bfloat16 [2, 512, 2048], P('batch', 'ctx', 'fsdp')
- grad_w: float32 [4096, 256], P(('ctx', 'batch'), 'fsdp')
All inputs are finite; a program needn't handle non-finite values.
Results may differ from a plain program's by a relative error of at most 0.013.
Values may be sent and summed in bfloat16 or wider, within the bound.
A program may use at most 64 MiB of HBM per device.

v0:
```python
import jax
import jax.numpy as jnp
import numpy as np
from jax import lax
from jax.sharding import PartitionSpec as P

F = 16
E = 256
CONV = 3


eps_norm = 1e-05
highest = lax.Precision.HIGHEST


def from_behind(value, axis, by):
    size = lax.axis_size(axis)
    pairs = [(i, i + by) for i in range(size) if 0 <= i + by < size]
    return lax.ppermute(value, axis, pairs)


def entering(value, axis, combine, identity, reverse):
    size, here = (lax.axis_size(axis), lax.axis_index(axis))
    everything = lax.all_gather(
        value.astype(jnp.bfloat16 if value.dtype == jnp.float32 else value.dtype), axis
    )
    start = jnp.broadcast_to(jnp.asarray(identity, value.dtype), value.shape)

    def turn(k, before):
        at = size - 1 - k if reverse else k
        reached = at > here if reverse else at < here
        new = combine(before, everything[at].astype(value.dtype))
        return jnp.where(reached, new, before)

    return lax.fori_loop(0, size, turn, start)


def expand_tables():
    leading_table = np.zeros((F, F * F), np.float32)
    trailing_table = np.zeros((F, F * F), np.float32)
    for first_at in range(F):
        for second_at in range(F):
            leading_table[first_at, first_at * F + second_at] = 1.0
            trailing_table[second_at, first_at * F + second_at] = 1.0
    return (jnp.asarray(leading_table), jnp.asarray(trailing_table))


def features(vector, leading_table, trailing_table):
    leading = vector.shape[:-1]
    first_rep = jnp.einsum("htf,fk->htk", vector, leading_table, precision=highest)
    second_rep = jnp.einsum("htf,fk->htk", vector, trailing_table, precision=highest)
    constant = jnp.ones(leading + (1,), jnp.float32)
    return jnp.concatenate(
        [constant, vector * F ** (-0.25), first_rep * second_rep * (2.0 * F) ** (-0.5)], axis=-1
    )


def features_back(vector, upstream, leading_table, trailing_table):
    linear = upstream[..., 1 : 1 + F]
    square = upstream[..., 1 + F :]
    first_rep = jnp.einsum("htf,fk->htk", vector, leading_table, precision=highest)
    second_rep = jnp.einsum("htf,fk->htk", vector, trailing_table, precision=highest)
    paired = jnp.einsum("htk,fk->htf", square * second_rep, leading_table, precision=highest)
    paired = paired + jnp.einsum(
        "htk,fk->htf", square * first_rep, trailing_table, precision=highest
    )
    return linear * F ** (-0.25) + paired * (2.0 * F) ** (-0.5)


def pack_tables():
    full_rows = 1 + F + F * F
    packed_rows = 1 + F + F * (F + 1) // 2
    gather_table = np.zeros((packed_rows, full_rows), np.float32)
    spread_table = np.zeros((full_rows, packed_rows), np.float32)
    for feature in range(1 + F):
        gather_table[feature, feature] = 1.0
        spread_table[feature, feature] = 1.0
    position = 1 + F
    for leading_at in range(F):
        for trailing_at in range(leading_at, F):
            upper_row = 1 + F + leading_at * F + trailing_at
            lower_row = 1 + F + trailing_at * F + leading_at
            gather_table[position, upper_row] = 1.0
            if leading_at == trailing_at:
                spread_table[upper_row, position] = 1.0
            else:
                gather_table[position, lower_row] = 1.0
                spread_table[upper_row, position] = 0.5
                spread_table[lower_row, position] = 0.5
            position += 1
    return (jnp.asarray(gather_table), jnp.asarray(spread_table))


def add_terms(earlier, later_term):
    return earlier + later_term


def shards(inputs, values, w_qk, conv_qk, conv_v, d_attn):
    weights = lax.all_to_all(w_qk, "fsdp", split_axis=1, concat_axis=0, tiled=True)
    tokens = inputs[0]
    positions = tokens.shape[0]
    width_qk = weights.shape[1]
    heads = width_qk // (2 * F)
    leading_table, trailing_table = expand_tables()
    conv_all = jnp.concatenate([conv_qk, conv_v], axis=1)
    qk_raw = jnp.dot(tokens, weights, preferred_element_type=jnp.float32).astype(jnp.bfloat16)
    joined = jnp.concatenate([qk_raw, values[0]], axis=1)
    rim_rows = from_behind(joined[positions - (CONV - 1) :], "ctx", 1)
    extended = jnp.concatenate([rim_rows, joined], axis=0)
    running = jnp.zeros(joined.shape, jnp.float32)
    for offset in range(CONV):
        running = running + conv_all[offset] * extended[
            CONV - 1 - offset : CONV - 1 - offset + positions
        ].astype(jnp.float32)
    convolved = running.astype(jnp.bfloat16)
    paired = convolved[:, :width_qk].reshape(positions, heads, 2 * F).transpose(1, 0, 2)
    queries = paired[:, :, :F]
    key_rows = paired[:, :, F:]
    valued = convolved[:, width_qk:].reshape(positions, heads, E).transpose(1, 0, 2)
    query32 = queries.astype(jnp.float32)
    key32 = key_rows.astype(jnp.float32)
    value32 = valued.astype(jnp.float32)
    query_feat = features(query32, leading_table, trailing_table)
    key_feat = features(key32, leading_table, trailing_table)
    own_state = jnp.einsum("hpf,hpe->hfe", key_feat, value32, precision=highest)
    gather_table, spread_table = pack_tables()
    payload = jnp.einsum("gf,hfe->hge", gather_table, own_state, precision=highest)
    carried = entering(payload, "ctx", add_terms, jnp.zeros(payload.shape, jnp.float32), False)
    prior = jnp.einsum("fg,hge->hfe", spread_table, carried, precision=highest)
    dotted = jnp.einsum(
        "htf,hpf->htp", queries, key_rows, preferred_element_type=jnp.float32
    ) * F ** (-0.5)
    rows_at = lax.broadcasted_iota(jnp.int32, (positions, positions), 0)
    cols_at = lax.broadcasted_iota(jnp.int32, (positions, positions), 1)
    causal = (cols_at <= rows_at)[None]
    kernel_b = jnp.where(causal, 1.0 + dotted + 0.5 * dotted * dotted, 0.0).astype(jnp.bfloat16)
    mixed_out = jnp.einsum("htp,hpe->hte", kernel_b, valued, preferred_element_type=jnp.float32)
    mixed_out = mixed_out + jnp.einsum("htf,hfe->hte", query_feat, prior, precision=highest)
    scale_inv = lax.rsqrt(jnp.mean(mixed_out * mixed_out, axis=-1, keepdims=True) + eps_norm)
    normed = mixed_out * scale_inv
    attended = normed.astype(jnp.bfloat16).transpose(1, 0, 2).reshape(1, positions, heads * E)
    grad_in = d_attn[0].reshape(positions, heads, E).transpose(1, 0, 2).astype(jnp.float32)
    d_mixed = (
        scale_inv * (grad_in - normed * jnp.mean(grad_in * normed, axis=-1, keepdims=True))
    ).astype(jnp.bfloat16)
    d_mixed32 = d_mixed.astype(jnp.float32)
    own_grad = jnp.einsum("htf,hte->hfe", query_feat, d_mixed32, precision=highest)
    grad_payload = jnp.einsum("gf,hfe->hge", gather_table, own_grad, precision=highest)
    grad_carried = entering(
        grad_payload, "ctx", add_terms, jnp.zeros(grad_payload.shape, jnp.float32), True
    )
    later = jnp.einsum("fg,hge->hfe", spread_table, grad_carried, precision=highest)
    d_kernel = jnp.einsum("hte,hpe->htp", d_mixed, valued, preferred_element_type=jnp.float32)
    d_score = (jnp.where(causal, d_kernel * (1.0 + dotted), 0.0) * F ** (-0.5)).astype(jnp.bfloat16)
    d_query = jnp.einsum("htp,hpf->htf", d_score, key_rows, preferred_element_type=jnp.float32)
    d_query = d_query + features_back(
        query32,
        jnp.einsum("hte,hfe->htf", d_mixed32, prior, precision=highest),
        leading_table,
        trailing_table,
    )
    d_key = jnp.einsum("htp,htf->hpf", d_score, queries, preferred_element_type=jnp.float32)
    d_key = d_key + features_back(
        key32,
        jnp.einsum("hpe,hfe->hpf", value32, later, precision=highest),
        leading_table,
        trailing_table,
    )
    d_valued = jnp.einsum("htp,hte->hpe", kernel_b, d_mixed, preferred_element_type=jnp.float32)
    d_valued = d_valued + jnp.einsum("hpf,hfe->hpe", key_feat, later, precision=highest)
    d_paired = (
        jnp.concatenate([d_query, d_key], axis=2).transpose(1, 0, 2).reshape(positions, width_qk)
    )
    d_joined = jnp.concatenate(
        [d_paired, d_valued.transpose(1, 0, 2).reshape(positions, heads * E)], axis=1
    )
    next_rows = from_behind(d_joined[: CONV - 1], "ctx", -1)
    grad_ext = jnp.concatenate([d_joined, next_rows], axis=0)
    running = jnp.zeros(d_joined.shape, jnp.float32)
    for offset in range(CONV):
        running = running + conv_all[offset] * grad_ext[offset : offset + positions]
    grad_v = running[:, width_qk:].astype(jnp.bfloat16).reshape(1, positions, heads * E)
    d_qk = running[:, :width_qk].astype(jnp.bfloat16)
    ctx_count = lax.axis_size("ctx")
    batch_count = lax.axis_size("batch")
    grad_scale = float(positions * ctx_count * batch_count) ** (-0.5)
    grad_w = lax.psum_scatter(
        lax.dot_general(tokens, d_qk, (((0,), (0,)), ((), ())), preferred_element_type=jnp.float32),
        ("ctx", "batch"),
        scatter_dimension=0,
        tiled=True,
    )
    return (attended, grad_v, grad_w * grad_scale)


def solution(mesh):
    in_specs = (
        P("batch", "ctx", None),
        P("batch", "ctx", "fsdp"),
        P("fsdp", None),
        P(None, "fsdp"),
        P(None, "fsdp"),
        P("batch", "ctx", "fsdp"),
    )
    out_specs = (P("batch", "ctx", "fsdp"), P("batch", "ctx", "fsdp"), P(("ctx", "batch"), "fsdp"))
    return jax.shard_map(shards, mesh=mesh, in_specs=in_specs, out_specs=out_specs, check_vma=False)
```

profile of v0, /device:TPU:0, one launch (start us, length us, event | category | flops | bytes accessed | tf_op | source)
XLA Modules:
  0.0 131.6 jit_solution(6035819906465306905)
XLA Ops:
  7.2 2.1 %copy.40 = bf16[1024,256]{0,1:T(8,128)(2,1)} copy(bf16[1024,256]{1,0:T(8,128)(2,1)} %param.16) | data formatting | bytes 1048576 | tf_op args[2]
  9.3 6.4 %all-to-all-start = ((bf16[1024,4,64]{0,2,1:T(8,128)(2,1)}), bf16[1024,4,64]{0,2,1:T(8,128)(2,1)S(1)}, u32[]{:S(2)}, u32[]{:S(2)}) async-start(bf16[1024,4,64]{0,2,1:T(8,128)(2,1)} %bitcast.1), calls=%async_computation | async-start | bytes 1048576 | tf_op jit(solution)/shard_map/all_to_all | solution.py:99
  15.9 14.3 %all-to-all-done = bf16[1024,4,64]{0,2,1:T(8,128)(2,1)S(1)} async-done(((bf16[1024,4,64]{0,2,1:T(8,128)(2,1)}), bf16[1024,4,64]{0,2,1:T(8,128)(2,1)S(1)}, u32[]{:S(2)}, u32[]{:S(2)}) %all-to-all-start) | async-done | bytes 524320 | tf_op jit(solution)/shard_map/all_to_all | solution.py:99
  30.9 1.3 collective-permute-start
  32.4 0.8 copy.50
  33.2 0.7 copy-done.34
  35.6 0.7 copy-done.15
  38.6 1.0 multiply_multiply_fusion
  39.6 0.7 fusion.14
  40.5 0.8 fusion.1
  41.3 10.9 %all-gather = bf16[8,153,256]{2,1,0:T(8,128)(2,1)S(1)} all-gather(bf16[2,153,256]{2,1,0:T(8,128)(2,1)S(1)} %fusion.1), channel_id=2, replica_groups=mesh['ctx'=4,'fsdp'=4,'batch'=2] {'ctx'}, dimensions={0}, use_global_device_ids=true | all-gather | bytes 783360 | tf_op jit(solution)/shard_map/all_gather | solution.py:24
  52.8 1.0 multiply_multiply_fusion.1
  54.0 0.8 fusion.63
  54.8 0.7 fusion.16
  56.9 0.7 copy-done.5
  57.6 0.7 fusion.15
  58.5 1.1 fusion.64
  59.6 0.8 fusion.2
  60.4 8.0 %all-gather.1 = bf16[8,153,256]{2,1,0:T(8,128)(2,1)S(1)} all-gather(bf16[2,153,256]{2,1,0:T(8,128)(2,1)S(1)} %fusion.2), channel_id=3, replica_groups=mesh['ctx'=4,'fsdp'=4,'batch'=2] {'ctx'}, dimensions={0}, use_global_device_ids=true | all-gather | bytes 783360 | tf_op jit(solution)/shard_map/all_gather | solution.py:24
  68.4 0.6 while.31
  69.1 1.7 %fusion.65 = f32[2,256,273]{1,2,0:T(8,128)S(1)} fusion(f32[2,153,256]{2,1,0:T(8,128)S(1)} %get-tuple-element.193, f32[273,153,1]{0,1,2:T(8,128)} %constant.113), kind=kOutput, calls=%fused_computation.108 | convolution fusion | flops 256628736 | bytes 1039524 | tf_op jit(solution)/shard_map/fg,hge->hfe/dot_general | solution.py:152
  71.7 1.4 %fusion.13 = f32[2,128,256]{2,1,0:T(8,128)} fusion(f32[2,256,273]{1,2,0:T(8,128)S(1)} %fusion.65, f32[2,128,256]{2,1,0:T(8,128)S(1)} %get-tuple-element.253, f32[2,128,16]{2,1,0:T(8,128)S(1)} %copy-done.3, f32[273]{0:T(512)S(1)} %copy-done.25), kind=kOutput, calls=%fused_computation.30 | convolution fusion | flops 214835712 | bytes 1100868 | tf_op jit(solution)/shard_map/hpf,hfe->hpe/dot_general | solution.py:170
  75.0 1.1 fusion.7
  76.7 0.7 copy-done.8
  77.7 0.8 copy-done.9
  78.9 1.3 collective-permute-start.1
  80.2 2.2 %collective-permute-done.1 = f32[2,576]{0,1:T(8,128)S(1)} collective-permute-done((f32[2,576]{0,1:T(8,128)S(1)}, f32[2,576]{0,1:T(8,128)S(1)}, u32[]{:S(2)}, u32[]{:S(2)}) %collective-permute-start.1) | collective-permute-done | bytes 4640 | tf_op jit(solution)/shard_map/ppermute | solution.py:19
  83.0 1.3 convolution_bitcast_fusion
  85.2 0.8 copy.57
  85.9 0.8 copy.58
  86.7 36.5 %reduce-scatter.2.cloned.1.call-done = f32[512,64]{0,1:T(8,128)} async-done(((f32[4096,64]{0,1:T(8,128)}), f32[512,64]{0,1:T(8,128)}) %reduce-scatter.2.cloned.1.call-update) | async-done | bytes 131088 | tf_op jit(solution)/shard_map/reduce_scatter | solution.py:187
  123.2 1.6 %broadcast_multiply_fusion = f32[512,64]{0,1:T(8,128)} fusion(f32[512,64]{0,1:T(8,128)} %reduce-scatter.2.cloned.1.call-done), kind=kLoop, calls=%fused_computation.73 | loop fusion | flops 32768 | bytes 262144 | tf_op jit(solution)/shard_map/mul | solution.py:193
  (124 shorter events, 13.8 us)
Async XLA Ops:
  7.2 23.1 %copy-start = (bf16[1,128,4096]{2,1,0:T(8,128)(2,1)S(1)}, bf16[1,128,4096]{2,1,0:T(8,128)(2,1)}, u32[]{:S(2)}) copy-start(bf16[1,128,4096]{2,1,0:T(8,128)(2,1)} %param.14) | copy-start | bytes 3145732
  9.3 6.5 %copy-start.22 = (bf16[1,128,512]{2,1,0:T(8,128)(2,1)S(1)}, bf16[1,128,512]{2,1,0:T(8,128)(2,1)}, u32[]{:S(2)}) copy-start(bf16[1,128,512]{2,1,0:T(8,128)(2,1)} %param.15) | copy-start | bytes 393220
  9.3 20.9 %all-to-all-start = ((bf16[1024,4,64]{0,2,1:T(8,128)(2,1)}), bf16[1024,4,64]{0,2,1:T(8,128)(2,1)S(1)}, u32[]{:S(2)}, u32[]{:S(2)}) async-start(bf16[1024,4,64]{0,2,1:T(8,128)(2,1)} %bitcast.1), calls=%async_computation | async-start | bytes 1048576 | tf_op jit(solution)/shard_map/all_to_all | solution.py:99
  15.8 107.4 %reduce-scatter.2.cloned.1.call-start = ((), (), s32[]{:S(2)}) async-start(), calls=%async_computation.2 | async-start | bytes 1179648 | tf_op jit(solution)/shard_map/reduce_scatter | solution.py:187
  15.9 39.6 %copy-start.19 = (pred[128,128]{1,0:T(8,128)(4,1)}, pred[128,128]{1,0:T(8,128)(4,1)S(1)}, u32[]{:S(2)}) copy-start(pred[128,128]{1,0:T(8,128)(4,1)S(1)} %iota_compare_fusion) | copy-start | bytes 49156
  30.8 1.4 %copy-start.23 = (bf16[1,128,512]{2,1,0:T(8,128)(2,1)S(1)}, bf16[1,128,512]{2,1,0:T(8,128)(2,1)}, u32[]{:S(2)}) copy-start(bf16[1,128,512]{2,1,0:T(8,128)(2,1)} %param.19) | copy-start | bytes 393220
  30.9 3.1 %collective-permute-start = (bf16[2,576]{0,1:T(8,128)(2,1)S(1)}, bf16[2,576]{0,1:T(8,128)(2,1)S(1)}, u32[]{:S(2)}, u32[]{:S(2)}) collective-permute-start(bf16[2,576]{0,1:T(8,128)(2,1)S(1)} %fusion.36), channel_id=1, source_target_pairs={{0,8},{8,16},{16,24},{1,9},{9,17},{17,25},{2,10},{10,18},{18,26},{... | collective-permute-start | bytes 6920 | tf_op jit(solution)/shard_map/ppermute | solution.py:19
  32.4 0.8 copy-start.32
  33.9 23.0 %copy-start.24 = (f32[273]{0:T(512)}, f32[273]{0:T(512)S(1)}, u32[]{:S(2)}) copy-start(f32[273]{0:T(512)S(1)} %pad.10.clone) | copy-start | bytes 3280
  35.6 0.7 copy-start.15
  37.0 0.9 slice-start
  37.3 2.3 %copy-start.2 = (f32[2,128,16]{2,1,0:T(8,128)}, f32[2,128,16]{2,1,0:T(8,128)S(1)}, u32[]{:S(2)}) copy-start(f32[2,128,16]{2,1,0:T(8,128)S(1)} %copy.45) | copy-start | bytes 49156
  39.6 0.9 copy-start.12
  52.8 1.1 copy-start.11
  54.0 0.8 copy-start.4
  55.5 1.0 copy-start.1
  56.7 0.9 copy-start.5
  58.5 1.1 copy-start.13
  70.8 0.9 copy-start.3
  70.8 0.9 copy-start.25
  71.7 1.4 %copy-start.7 = (f32[2,128,273]{1,2,0:T(8,128)}, f32[2,128,273]{1,2,0:T(8,128)S(1)}, u32[]{:S(2)}) copy-start(f32[2,128,273]{1,2,0:T(8,128)S(1)} %fusion.37) | copy-start | bytes 838660
  73.2 0.7 copy-start.18
  73.9 0.9 copy-start.10
  74.2 0.8 copy-start.16
  75.0 1.3 copy-start.6
  76.4 1.0 copy-start.8
  76.4 0.9 copy-start.21
  77.6 1.0 copy-start.9
  78.9 3.6 %copy-start.27 = (f32[576]{0:T(1024)S(1)}, f32[576]{0:T(1024)}, u32[]{:S(2)}) copy-start(f32[576]{0:T(1024)} %copy-done.26) | copy-start | bytes 6916
  78.9 3.6 %copy-start.29 = (f32[576]{0:T(1024)S(1)}, f32[576]{0:T(1024)}, u32[]{:S(2)}) copy-start(f32[576]{0:T(1024)} %copy-done.28) | copy-start | bytes 6916
  78.9 3.6 %copy-start.31 = (f32[576]{0:T(1024)S(1)}, f32[576]{0:T(1024)}, u32[]{:S(2)}) copy-start(f32[576]{0:T(1024)} %copy-done.30) | copy-start | bytes 6916
  78.9 3.5 %collective-permute-start.1 = (f32[2,576]{0,1:T(8,128)S(1)}, f32[2,576]{0,1:T(8,128)S(1)}, u32[]{:S(2)}, u32[]{:S(2)}) collective-permute-start(f32[2,576]{0,1:T(8,128)S(1)} %fusion.21), channel_id=1, source_target_pairs={{8,0},{16,8},{24,16},{9,1},{17,9},{25,17},{10,2},{18,10},{26,18},{... | collective-permute-start | bytes 13832 | tf_op jit(solution)/shard_map/ppermute | solution.py:19
  (8 other events, 5.2 us)
Sparse Core Ops, SparseCore 0:
  84.4 38.7 reduce-scatter.1
where the time goes:
time: 132 us
  waiting for transfers between devices  53 us (40%)
  blocking collectives  18.9 us (14%)
  matrix products  16.7 us (13%)
  between operations  14.6 us (11%)
  local copies, waits for them, and re-layouts  14.3 us (11%)
  starting transfers between devices  9.04 us (7%)
  other arithmetic  4.93 us (4%)
    reduce_scatter x1, waiting for transfers between devices, shards(): lax.psum_scatter(lax.dot_general(tokens, d_qk, (((0,), (0,)), ((), ())),...  36.5 us
    all_gather x2, blocking collectives, entering(): lax.all_gather(value.astype(jnp.bfloat16 if value.dtype == jnp.float32 el...  18.9 us
    all_to_all x1, waiting for transfers between devices, shards(): lax.all_to_all(w_qk, 'fsdp', split_axis=1, concat_axis=0, tiled=True)  14.3 us
    unnamed x77, local copies, waits for them, and re-layouts  12.2 us
    all_to_all x1, starting transfers between devices, shards(): lax.all_to_all(w_qk, 'fsdp', split_axis=1, concat_axis=0, tiled=True)  6.45 us
  transfers between devices with their start and end apart: 4, of which 3 were waited for; matrix products, arithmetic and copies ran while one was open for 2% of the time, Pallas kernels for 0%

commit v1 on v0

v1 whole, which is shorter than its diff:
```python
import functools

import jax
import jax.numpy as jnp
from jax import lax
from jax.experimental import pallas as pl
from jax.experimental.pallas import tpu as pltpu
from jax.sharding import PartitionSpec as P

F = 16
E = 256
CONV = 3
PACKED = 8 * F + F // 2 + 8 + F
RIM_V = 16
RIM = 8

eps_norm = 1e-05
MESH = pl.DeviceIdType.MESH
bf16, f32 = jnp.bfloat16, jnp.float32


def dot(a, b):
    return jnp.dot(a, b, preferred_element_type=f32)


def dot_nt(a, b):
    return lax.dot_general(a, b, (((1,), (1,)), ((), ())), preferred_element_type=f32)


def turned(rows, by):
    if by == 0:
        return rows
    return jnp.concatenate([rows[by:], rows[:by]], axis=0)


def features(vec):
    positions = vec.shape[1]
    rows = [vec * vec * (2.0 * F) ** (-0.5)]
    scaled = vec * F ** (-0.5)
    for by in range(1, F // 2):
        rows.append(scaled * turned(vec, by))
    rows.append(scaled[: F // 2] * vec[F // 2 :])
    first = lax.broadcasted_iota(jnp.int32, (8, positions), 0) == 0
    rows.append(jnp.where(first, 1.0, 0.0).astype(f32))
    rows.append(vec * F ** (-0.25))
    return jnp.concatenate(rows, axis=0)


def features_back(vec, up):
    half = F // 2
    total = vec * up[:F] * (2.0 * (2.0 * F) ** (-0.5))
    total = total + up[8 * F + half + 8 :] * F ** (-0.25)
    pairs = jnp.zeros_like(vec)
    for by in range(1, half):
        part = up[by * F : (by + 1) * F]
        pairs = pairs + turned(vec, by) * part + turned(vec * part, F - by)
    part = up[half * F : half * F + half]
    pairs = pairs + jnp.concatenate([vec[half:] * part, vec[:half] * part], axis=0)
    return total + pairs * F ** (-0.5)


def column_of(row):
    n = row.shape[1]
    same = lax.broadcasted_iota(jnp.int32, (n, n), 0) == lax.broadcasted_iota(jnp.int32, (n, n), 1)
    return jnp.sum(jnp.where(same, row, 0.0), axis=1, keepdims=True)


def body(
    dims, tokens, values, weights, conv_qk, conv_v, d_attn,
    attended, grad_v, grad_w,
    part_t, part_in, rim_out, rim_in, rim_t, vrim_in, ext_v, conv_b,
    state_out, state_in, prior, grad_out, grad_in, later, mixed_b,
    dv_ext, dqk_out, dqk_in, x_in, dq_all,
    part_ss, part_rs, rim_ss, rim_rs, vrim_ss, vrim_rs, state_ss, state_rs,
    grad_ss, grad_rs, dv_ss, dv_rs, dqk_ss, dqk_rs, x_ss, x_rs, dq_ss, dq_rs,
):
    n_ctx, n_fsdp, n_batch, gather = dims
    ctx, fsdp, batch = lax.axis_index("ctx"), lax.axis_index("fsdp"), lax.axis_index("batch")
    positions = tokens.shape[0]
    depth = weights.shape[0]
    width = conv_qk.shape[1]
    heads = width // (2 * F)
    wide = values.shape[1]
    group = n_ctx * n_batch
    me = ctx * n_batch + batch
    inner, outer = ctx > 0, ctx < n_ctx - 1

    def copy(src, dst, ss, rs, to):
        return pltpu.make_async_remote_copy(
            src_ref=src, dst_ref=dst, send_sem=ss, recv_sem=rs, device_id=to, device_id_type=MESH
        )

    bar = pltpu.get_barrier_semaphore()

    def greet(to):
        pl.semaphore_signal(bar, inc=1, device_id=to, device_id_type=MESH)

    for r in range(1, n_fsdp):
        greet((ctx, lax.rem(fsdp + r, n_fsdp), batch))
    if gather:
        for r in range(1, group):
            peer = lax.rem(me + r, group)
            greet((peer // n_batch, fsdp, lax.rem(peer, n_batch)))
        count = group - 1 + n_fsdp - 1
        same = range(1, n_fsdp)
    else:
        for r in range(1, n_ctx):
            greet((lax.rem(ctx + r, n_ctx), fsdp, batch))
        count = n_ctx - 1 + n_fsdp - 1
        same = range(1, n_fsdp)

    @pl.when(inner)
    def _():
        for r in same:
            greet((ctx - 1, lax.rem(fsdp + r, n_fsdp), batch))

    @pl.when(outer)
    def _():
        for r in same:
            greet((ctx + 1, lax.rem(fsdp + r, n_fsdp), batch))

    columns = pl.ds(pl.multiple_of(fsdp * depth, depth), depth)
    part = dot(tokens[:, columns], weights[...])
    part_t[...] = part.T.reshape(part_t.shape)
    rim_out[...] = part[positions - RIM :]
    pl.semaphore_wait(
        bar, count + jnp.where(inner, n_fsdp - 1, 0) + jnp.where(outer, n_fsdp - 1, 0)
    )

    def part_copy(r):
        peer = lax.rem(fsdp + r, n_fsdp)
        return copy(part_t.at[peer], part_in.at[fsdp], part_ss.at[r], part_rs.at[fsdp], (ctx, peer, batch))

    def rim_copy(r):
        peer = lax.rem(fsdp + r, n_fsdp)
        return copy(rim_out, rim_in.at[fsdp], rim_ss.at[r], rim_rs.at[fsdp], (ctx + 1, peer, batch))

    def vrim_copy():
        return copy(values.at[pl.ds(positions - RIM_V, RIM_V)], vrim_in, vrim_ss, vrim_rs, (ctx + 1, fsdp, batch))

    for r in range(1, n_fsdp):
        part_copy(r).start()

    @pl.when(outer)
    def _():
        for r in range(n_fsdp):
            rim_copy(r).start()
        vrim_copy().start()

    cols = grad_w.shape[1]

    def x_copy(r):
        peer = lax.rem(me + r, group)
        return copy(
            tokens.at[:, pl.ds(pl.multiple_of(peer * cols, cols), cols)],
            x_in.at[me], x_ss.at[r], x_rs.at[me],
            (peer // n_batch, fsdp, lax.rem(peer, n_batch)),
        )

    if gather:
        for r in range(1, group):
            x_copy(r).start()

    @pl.when(inner)
    def _():
        vrim_copy().wait_recv()
        ext_v[0:RIM_V] = vrim_in[...].astype(f32)

    @pl.when(jnp.logical_not(inner))
    def _():
        ext_v[0:RIM_V] = jnp.zeros((RIM_V, wide), f32)

    ext_v[RIM_V:] = values[...].astype(f32)
    running = conv_v[0:1] * ext_v[RIM_V:]
    for j in range(1, CONV):
        running = running + conv_v[j : j + 1] * ext_v[RIM_V - j : RIM_V - j + positions]
    conv_b[...] = running.astype(bf16)

    for r in range(1, n_fsdp):
        src = lax.rem(fsdp + r, n_fsdp)
        copy(part_in.at[src], part_in.at[src], part_ss.at[r], part_rs.at[src], (ctx, src, batch)).wait_recv()
    part_in[fsdp] = part_t[fsdp]
    raw = part_in[0]
    for s in range(1, n_fsdp):
        raw = raw + part_in[s]
    raw = raw.astype(bf16).astype(f32)

    @pl.when(inner)
    def _():
        for s in range(n_fsdp):
            copy(rim_in.at[s], rim_in.at[s], rim_ss.at[s], rim_rs.at[s], (ctx - 1, s, batch)).wait_recv()
        rows = rim_in[0]
        for s in range(1, n_fsdp):
            rows = rows + rim_in[s]
        rows = rows.astype(bf16).astype(f32)
        block = jnp.concatenate([jnp.zeros((positions - RIM, rows.shape[1]), f32), rows], axis=0)
        rim_t[...] = block.T

    @pl.when(jnp.logical_not(inner))
    def _():
        rim_t[...] = jnp.zeros(rim_t.shape, f32)

    before = rim_t[pl.ds(pl.multiple_of(fsdp * width, width), width), :]
    lane = lax.broadcasted_iota(jnp.int32, (width, positions), 1)
    taps = [column_of(conv_qk[j : j + 1]) for j in range(CONV)]
    running = taps[0] * raw
    for j in range(1, CONV):
        moved = jnp.where(lane < j, pltpu.roll(before, j, 1), pltpu.roll(raw, j, 1))
        running = running + taps[j] * moved
    qk_t = running.astype(bf16).astype(f32)
    qk = qk_t.T.astype(bf16)

    q_t = [qk_t[h * 2 * F : h * 2 * F + F] for h in range(heads)]
    k_t = [qk_t[h * 2 * F + F : (h + 1) * 2 * F] for h in range(heads)]
    fk_t = [features(k) for k in k_t]
    for h in range(heads):
        value = conv_b[:, h * E : (h + 1) * E]
        state_out[h] = dot(fk_t[h].astype(bf16), value).astype(bf16)

    def state_copy(r):
        return copy(state_out, state_in.at[ctx], state_ss.at[r], state_rs.at[ctx], (ctx + r, fsdp, batch))

    for r in range(1, n_ctx):
        @pl.when(ctx + r < n_ctx)
        def _():
            state_copy(r).start()

    fq_t = [features(q) for q in q_t]
    fq = [x.T.astype(bf16) for x in fq_t]
    fk = [x.T.astype(bf16) for x in fk_t]
    at_row = lax.broadcasted_iota(jnp.int32, (positions, positions), 0)
    at_col = lax.broadcasted_iota(jnp.int32, (positions, positions), 1)
    scores_t, kernels_t, local = [], [], []
    for h in range(heads):
        q, k = qk[:, h * 2 * F : h * 2 * F + F], qk[:, h * 2 * F + F : (h + 1) * 2 * F]
        score = dot(q, k_t[h].astype(bf16)) * F ** (-0.5)
        kernel = jnp.where(at_col <= at_row, 1.0 + score + 0.5 * score * score, 0.0).astype(bf16)
        local.append(dot(kernel, conv_b[:, h * E : (h + 1) * E]))
        score_t = dot(k, q_t[h].astype(bf16)) * F ** (-0.5)
        scores_t.append(score_t)
        kernels_t.append(
            jnp.where(at_row <= at_col, 1.0 + score_t + 0.5 * score_t * score_t, 0.0).astype(bf16)
        )

    prior[...] = jnp.zeros(prior.shape, f32)
    for s in range(n_ctx - 1):
        @pl.when(s < ctx)
        def _():
            copy(state_in.at[s], state_in.at[s], state_ss.at[s], state_rs.at[s], (s, fsdp, batch)).wait_recv()
            prior[...] += state_in[s].astype(f32)
    prior_b = [prior[h].astype(bf16) for h in range(heads)]
    for h in range(heads):
        lanes = slice(h * E, (h + 1) * E)
        mixed = local[h] + dot(fq[h], prior_b[h])
        inv = lax.rsqrt(jnp.mean(mixed * mixed, axis=-1, keepdims=True) + eps_norm)
        normed = mixed * inv
        attended[:, lanes] = normed.astype(bf16)
        g = d_attn[:, lanes].astype(f32)
        d_mixed = (inv * (g - normed * jnp.mean(g * normed, axis=-1, keepdims=True))).astype(bf16)
        mixed_b[:, lanes] = d_mixed
        grad_out[h] = dot(fq_t[h].astype(bf16), d_mixed).astype(bf16)

    def grad_copy(r):
        return copy(grad_out, grad_in.at[ctx], grad_ss.at[r], grad_rs.at[ctx], (ctx - r, fsdp, batch))

    for r in range(1, n_ctx):
        @pl.when(ctx - r >= 0)
        def _():
            grad_copy(r).start()

    d_q, d_k, d_v = [], [], []
    for h in range(heads):
        lanes = slice(h * E, (h + 1) * E)
        d_mixed, value = mixed_b[:, lanes], conv_b[:, lanes]
        d_kernel_t = dot_nt(value, d_mixed)
        d_score_t = jnp.where(
            at_row <= at_col, d_kernel_t * (1.0 + scores_t[h]), 0.0
        ) * F ** (-0.5)
        d_score_t = d_score_t.astype(bf16)
        d_q.append(
            dot(k_t[h].astype(bf16), d_score_t) + features_back(q_t[h], dot_nt(prior_b[h], d_mixed))
        )
        d_k.append(dot_nt(q_t[h].astype(bf16), d_score_t))
        d_v.append(dot(kernels_t[h], d_mixed))

    later[...] = jnp.zeros(later.shape, f32)
    for s in range(1, n_ctx):
        @pl.when(s > ctx)
        def _():
            copy(grad_in.at[s], grad_in.at[s], grad_ss.at[s], grad_rs.at[s], (s, fsdp, batch)).wait_recv()
            later[...] += grad_in[s].astype(f32)
    rows = []
    for h in range(heads):
        lanes = slice(h * E, (h + 1) * E)
        later_b = later[h].astype(bf16)
        back = features_back(k_t[h], dot_nt(later_b, conv_b[:, lanes]))
        rows += [d_q[h], d_k[h] + back]
        dv_ext[0:positions, lanes] = d_v[h] + dot(fk[h], later_b)
    d_qk_t = jnp.concatenate(rows, axis=0)
    dqk_out[...] = d_qk_t

    def dv_copy():
        return copy(
            dv_ext.at[pl.ds(0, RIM)], dv_ext.at[pl.ds(positions, RIM)], dv_ss, dv_rs, (ctx - 1, fsdp, batch)
        )

    def dqk_copy():
        return copy(dqk_out, dqk_in, dqk_ss, dqk_rs, (ctx - 1, fsdp, batch))

    @pl.when(inner)
    def _():
        dqk_copy().start()
        dv_copy().start()

    @pl.when(outer)
    def _():
        dqk_copy().wait_recv()

    @pl.when(jnp.logical_not(outer))
    def _():
        dqk_in[...] = jnp.zeros(dqk_in.shape, f32)
        dv_ext[positions:] = jnp.zeros((RIM, wide), f32)

    after = dqk_in[...]
    running = taps[0] * d_qk_t
    for j in range(1, CONV):
        moved = jnp.where(
            lane >= positions - j, pltpu.roll(after, positions - j, 1), pltpu.roll(d_qk_t, positions - j, 1)
        )
        running = running + taps[j] * moved
    d_pre = running.astype(bf16)

    def dq_copy(r):
        peer = lax.rem(me + r, group)
        return copy(
            dq_all.at[me], dq_all.at[me], dq_ss.at[r], dq_rs.at[me],
            (peer // n_batch, fsdp, lax.rem(peer, n_batch)),
        )

    if gather:
        dq_all[me] = d_pre
        for r in range(1, group):
            dq_copy(r).start()
    else:
        grad_w[...] = d_pre

    @pl.when(outer)
    def _():
        dv_copy().wait_recv()

    running = conv_v[0:1] * dv_ext[0:positions]
    for j in range(1, CONV):
        running = running + conv_v[j : j + 1] * dv_ext[j : j + positions]
    grad_v[...] = running.astype(bf16)

    if gather:
        total = dot(d_pre, tokens[:, pl.ds(pl.multiple_of(me * cols, cols), cols)])
        for r in range(1, group):
            src = lax.rem(me + r, group)
            to = (src // n_batch, fsdp, lax.rem(src, n_batch))
            copy(x_in.at[src], x_in.at[src], x_ss.at[r], x_rs.at[src], to).wait_recv()
            copy(dq_all.at[src], dq_all.at[src], dq_ss.at[r], dq_rs.at[src], to).wait_recv()
            total = total + dot(dq_all[src], x_in[src])
        grad_w[...] = total * float(positions * group) ** (-0.5)
        for r in range(1, group):
            x_copy(r).wait_send()
            dq_copy(r).wait_send()

    for r in range(1, n_fsdp):
        part_copy(r).wait_send()

    @pl.when(outer)
    def _():
        for r in range(n_fsdp):
            rim_copy(r).wait_send()
        vrim_copy().wait_send()

    @pl.when(inner)
    def _():
        dqk_copy().wait_send()
        dv_copy().wait_send()

    for r in range(1, n_ctx):
        @pl.when(ctx + r < n_ctx)
        def _():
            state_copy(r).wait_send()

        @pl.when(ctx - r >= 0)
        def _():
            grad_copy(r).wait_send()


def shards(dims, inputs, values, w_qk, conv_qk, conv_v, d_attn):
    n_ctx, n_fsdp, n_batch = dims
    tokens = inputs[0]
    positions, model = tokens.shape
    wide = values.shape[2]
    width = conv_qk.shape[1]
    heads = width // (2 * F)
    group = n_ctx * n_batch
    cols = model // group
    gather = cols % 128 == 0
    last = (width, cols) if gather else (width, positions)
    slots = group if gather else 1
    dma = pltpu.SemaphoreType.DMA
    state = (heads, PACKED, E)
    vmem = pl.BlockSpec(memory_space=pltpu.VMEM)
    scratch = [
        pltpu.VMEM((n_fsdp, width, positions), f32),
        pltpu.VMEM((n_fsdp, width, positions), f32),
        pltpu.VMEM((RIM, w_qk.shape[1]), f32),
        pltpu.VMEM((n_fsdp, RIM, w_qk.shape[1]), f32),
        pltpu.VMEM((w_qk.shape[1], positions), f32),
        pltpu.VMEM((RIM_V, wide), bf16),
        pltpu.VMEM((RIM_V + positions, wide), f32),
        pltpu.VMEM((positions, wide), bf16),
        pltpu.VMEM(state, bf16),
        pltpu.VMEM((n_ctx,) + state, bf16),
        pltpu.VMEM(state, f32),
        pltpu.VMEM(state, bf16),
        pltpu.VMEM((n_ctx,) + state, bf16),
        pltpu.VMEM(state, f32),
        pltpu.VMEM((positions, wide), bf16),
        pltpu.VMEM((positions + RIM, wide), f32),
        pltpu.VMEM((width, positions), f32),
        pltpu.VMEM((width, positions), f32),
        pltpu.VMEM((slots, positions, cols if gather else 128), bf16),
        pltpu.VMEM((slots, width, positions), bf16),
        dma((n_fsdp,)), dma((n_fsdp,)), dma((n_fsdp,)), dma((n_fsdp,)), dma, dma,
        dma((n_ctx,)), dma((n_ctx,)), dma((n_ctx,)), dma((n_ctx,)), dma, dma, dma, dma,
        dma((slots,)), dma((slots,)), dma((slots,)), dma((slots,)),
    ]
    attended, grad_v, tail = pl.pallas_call(
        functools.partial(body, (n_ctx, n_fsdp, n_batch, gather)),
        out_shape=(
            jax.ShapeDtypeStruct((positions, wide), bf16),
            jax.ShapeDtypeStruct((positions, wide), bf16),
            jax.ShapeDtypeStruct(last, f32 if gather else bf16),
        ),
        in_specs=[vmem] * 6,
        out_specs=(vmem,) * 3,
        scratch_shapes=scratch,
        compiler_params=pltpu.CompilerParams(
            collective_id=0, has_side_effects=True, vmem_limit_bytes=40 * 2**20
        ),
    )(tokens, values[0], w_qk, conv_qk, conv_v, d_attn[0])
    if gather:
        grad_w = tail.T
    else:
        grad_w = lax.psum_scatter(
            dot(tail, tokens).T, ("ctx", "batch"), scatter_dimension=0, tiled=True
        ) * float(positions * group) ** (-0.5)
    return (attended[None], grad_v[None], grad_w)


def solution(mesh):
    in_specs = (
        P("batch", "ctx", None),
        P("batch", "ctx", "fsdp"),
        P("fsdp", None),
        P(None, "fsdp"),
        P(None, "fsdp"),
        P("batch", "ctx", "fsdp"),
    )
    out_specs = (P("batch", "ctx", "fsdp"), P("batch", "ctx", "fsdp"), P(("ctx", "batch"), "fsdp"))
    dims = (mesh.shape["ctx"], mesh.shape["fsdp"], mesh.shape["batch"])
    return jax.shard_map(
        functools.partial(shards, dims), mesh=mesh, in_specs=in_specs, out_specs=out_specs, check_vma=False
    )
```

time: 132 us -> 48.7 us (0.37)
  waiting for transfers between devices: 53 us -> 0 us
  Pallas kernels: 0 us -> 40.3 us
  blocking collectives: 18.9 us -> 0 us
  matrix products: 16.7 us -> 0 us
  between operations: 14.6 us -> 0.65 us
  starting transfers between devices: 9.04 us -> 0 us
  local copies, waits for them, and re-layouts: 14.3 us -> 7.41 us
  other arithmetic: 4.93 us -> 0 us
    pallas_call x0 -> x1, Pallas kernels: none -> 40.3 us  [shards(): pl.pallas_call(functools.partial(body, (n_ctx, n_fsdp, n_batch, gather)),...]
    reduce_scatter x1 -> x0, waiting for transfers between devices: 36.5 us -> none  [shards(): lax.psum_scatter(lax.dot_general(tokens, d_qk, (((0,), (0,)), ((), ())),...]
    all_gather x2 -> x0, blocking collectives: 18.9 us -> none  [entering(): lax.all_gather(value.astype(jnp.bfloat16 if value.dtype == jnp.float32 el...]
    dot_general x26 -> x0, matrix products: 16.7 us -> none  [the longest x2 2.03 us: features(): jnp.einsum('htf,fk->htk', vector, leading_table, precision=highest)]
    all_to_all x1 -> x0, waiting for transfers between devices: 14.3 us -> none  [shards(): lax.all_to_all(w_qk, 'fsdp', split_axis=1, concat_axis=0, tiled=True)]
    all_to_all x1 -> x0, starting transfers between devices: 6.45 us -> none  [shards(): lax.all_to_all(w_qk, 'fsdp', split_axis=1, concat_axis=0, tiled=True)]
    unnamed x77 -> x15, local copies, waits for them, and re-layouts: 12.2 us -> 7.41 us
    ppermute x2 -> x0, starting transfers between devices: 2.59 us -> none  [from_behind(): return lax.ppermute(value, axis, pairs)]
  transfers between devices with their start and end apart: 4 -> 0, of which waited for: 3 -> 0; matrix products, arithmetic and copies ran while one was open for 2% -> 0% of each run, Pallas kernels for 0% -> 0%
where the time goes in v1:
time: 48.7 us; the launch traced here: 48.4 us
  Pallas kernels  40.3 us (83%)
  local copies, waits for them, and re-layouts  7.41 us (15%)
  between operations  0.65 us (1%)
    pallas_call x1, Pallas kernels, shards(): pl.pallas_call(functools.partial(body, (n_ctx, n_fsdp, n_batch, gather)),...  40.3 us
    unnamed x15, local copies, waits for them, and re-layouts  7.41 us

profile of v1, /device:TPU:0, one launch (start us, length us, event | category | flops | bytes accessed | tf_op | source)
XLA Modules:
  0.0 48.4 jit_solution(6166777731228164503)
XLA Ops:
  0.6 0.0 copy-start.5
  0.6 0.7 %copy-done.5 = f32[3,64]{1,0:T(4,128)S(1)} copy-done((f32[3,64]{1,0:T(4,128)S(1)}, f32[3,64]{1,0:T(4,128)}, u32[]{:S(2)}) %copy-start.5) | copy-done | bytes 792
  1.3 0.0 copy-start
  1.3 1.2 %copy-done = bf16[1,128,4096]{2,1,0:T(8,128)(2,1)S(1)} copy-done((bf16[1,128,4096]{2,1,0:T(8,128)(2,1)S(1)}, bf16[1,128,4096]{2,1,0:T(8,128)(2,1)}, u32[]{:S(2)}) %copy-start) | copy-done | bytes 1048600
  2.5 0.0 copy-start.1
  2.5 1.0 %copy-done.1 = bf16[1024,256]{1,0:T(8,128)(2,1)S(1)} copy-done((bf16[1024,256]{1,0:T(8,128)(2,1)S(1)}, bf16[1024,256]{1,0:T(8,128)(2,1)}, u32[]{:S(2)}) %copy-start.1) | copy-done | bytes 524312
  3.6 0.0 copy-start.2
  3.6 0.9 %copy-done.2 = bf16[1,128,512]{2,1,0:T(8,128)(2,1)S(1)} copy-done((bf16[1,128,512]{2,1,0:T(8,128)(2,1)S(1)}, bf16[1,128,512]{2,1,0:T(8,128)(2,1)}, u32[]{:S(2)}) %copy-start.2) | copy-done | bytes 131096
  4.5 0.0 copy-start.3
  4.5 0.9 %copy-done.3 = bf16[1,128,512]{2,1,0:T(8,128)(2,1)S(1)} copy-done((bf16[1,128,512]{2,1,0:T(8,128)(2,1)S(1)}, bf16[1,128,512]{2,1,0:T(8,128)(2,1)}, u32[]{:S(2)}) %copy-start.3) | copy-done | bytes 131096
  5.4 0.0 copy-start.4
  5.4 0.7 %copy-done.4 = f32[3,512]{1,0:T(4,128)S(1)} copy-done((f32[3,512]{1,0:T(4,128)S(1)}, f32[3,512]{1,0:T(4,128)}, u32[]{:S(2)}) %copy-start.4) | copy-done | bytes 6168
  6.1 40.3 %shard_map.85 = (bf16[128,512]{1,0:T(8,128)(2,1)S(1)}, bf16[128,512]{1,0:T(8,128)(2,1)S(1)}, f32[64,512]{1,0:T(8,128)S(1)}) custom-call(bf16[128,4096]{1,0:T(8,128)(2,1)S(1)} %bitcast.6, bf16[128,512]{1,0:T(8,128)(2,1)S(1)} %bitcast.7, bf16[1024,256]{1,0:T(8,128)(2,1)S(1)} %copy-done.1, f32[3,64]{1,0:T(4,128)S(1)} %copy-done.5, f32[3,512]{1,0:T(4,128)S(1)} %copy-done.4, ...), custom_call_target="tpu_custom_call" | custom-call | tf_op jit(solution)/shard_map/pallas_call | solution.py:433
  46.4 0.7 %copy.12 = bf16[1,128,512]{2,1,0:T(8,128)(2,1)} copy(bf16[1,128,512]{2,1,0:T(8,128)(2,1)S(1)} %bitcast.11) | data formatting | bytes 262144
  47.1 0.7 %copy.13 = bf16[1,128,512]{2,1,0:T(8,128)(2,1)} copy(bf16[1,128,512]{2,1,0:T(8,128)(2,1)S(1)} %bitcast.10) | data formatting | bytes 262144
  47.7 0.7 %copy.14 = f32[512,64]{0,1:T(8,128)} copy(f32[512,64]{0,1:T(8,128)S(1)} %bitcast.9) | data formatting | bytes 262144
Async XLA Ops:
  0.6 0.7 %copy-start.5 = (f32[3,64]{1,0:T(4,128)S(1)}, f32[3,64]{1,0:T(4,128)}, u32[]{:S(2)}) copy-start(f32[3,64]{1,0:T(4,128)} %conv_qk.1) | copy-start | bytes 2308
  1.3 1.2 %copy-start = (bf16[1,128,4096]{2,1,0:T(8,128)(2,1)S(1)}, bf16[1,128,4096]{2,1,0:T(8,128)(2,1)}, u32[]{:S(2)}) copy-start(bf16[1,128,4096]{2,1,0:T(8,128)(2,1)} %param.6) | copy-start | bytes 3145732
  2.5 1.0 %copy-start.1 = (bf16[1024,256]{1,0:T(8,128)(2,1)S(1)}, bf16[1024,256]{1,0:T(8,128)(2,1)}, u32[]{:S(2)}) copy-start(bf16[1024,256]{1,0:T(8,128)(2,1)} %weights.1) | copy-start | bytes 1572868
  3.6 0.9 %copy-start.2 = (bf16[1,128,512]{2,1,0:T(8,128)(2,1)S(1)}, bf16[1,128,512]{2,1,0:T(8,128)(2,1)}, u32[]{:S(2)}) copy-start(bf16[1,128,512]{2,1,0:T(8,128)(2,1)} %param.7) | copy-start | bytes 393220
  4.5 0.9 %copy-start.3 = (bf16[1,128,512]{2,1,0:T(8,128)(2,1)S(1)}, bf16[1,128,512]{2,1,0:T(8,128)(2,1)}, u32[]{:S(2)}) copy-start(bf16[1,128,512]{2,1,0:T(8,128)(2,1)} %param.11) | copy-start | bytes 393220
  5.4 0.7 %copy-start.4 = (f32[3,512]{1,0:T(4,128)S(1)}, f32[3,512]{1,0:T(4,128)}, u32[]{:S(2)}) copy-start(f32[3,512]{1,0:T(4,128)} %conv_v.1) | copy-start | bytes 18436

commit v2 on v1

--- a/solution.py
+++ b/solution.py
@@ -66,13 +66,15 @@
 
 
 def body(
-    dims, tokens, values, weights, conv_qk, conv_v, d_attn,
+    dims, tokens_h, values_h, weights_h, conv_qk_h, conv_v_h, d_attn_h,
     attended, grad_v, grad_w,
-    part_t, part_in, rim_out, rim_in, rim_t, vrim_in, ext_v, conv_b,
+    tokens, values, weights, conv_qk, conv_v, d_attn,
+    part_f, part_t, part_in, rim_out, rim_in, rim_t, vrim_in, ext_v, conv_b,
     state_out, state_in, prior, grad_out, grad_in, later, mixed_b,
     dv_ext, dqk_out, dqk_in, x_in, dq_all,
     part_ss, part_rs, rim_ss, rim_rs, vrim_ss, vrim_rs, state_ss, state_rs,
     grad_ss, grad_rs, dv_ss, dv_rs, dqk_ss, dqk_rs, x_ss, x_rs, dq_ss, dq_rs,
+    load_s, pass_s, back_s,
 ):
     n_ctx, n_fsdp, n_batch, gather = dims
     ctx, fsdp, batch = lax.axis_index("ctx"), lax.axis_index("fsdp"), lax.axis_index("batch")
@@ -119,14 +121,32 @@
         for r in same:
             greet((ctx + 1, lax.rem(fsdp + r, n_fsdp), batch))
 
+    loads = [
+        pltpu.make_async_copy(src, dst, load_s.at[i])
+        for i, (src, dst) in enumerate(
+            [
+                (weights_h, weights), (tokens_h, tokens), (values_h, values),
+                (conv_v_h, conv_v), (conv_qk_h, conv_qk), (d_attn_h, d_attn),
+            ]
+        )
+    ]
+    for load in loads:
+        load.start()
+    loads[0].wait()
+    loads[1].wait()
+
     columns = pl.ds(pl.multiple_of(fsdp * depth, depth), depth)
     part = dot(tokens[:, columns], weights[...])
-    part_t[...] = part.T.reshape(part_t.shape)
+    part_f[...] = part.T.reshape(part_f.shape)
+    part_t[...] = part_f[...].astype(bf16)
     rim_out[...] = part[positions - RIM :]
     pl.semaphore_wait(
         bar, count + jnp.where(inner, n_fsdp - 1, 0) + jnp.where(outer, n_fsdp - 1, 0)
     )
 
+    for load in loads[2:]:
+        load.wait()
+
     def part_copy(r):
         peer = lax.rem(fsdp + r, n_fsdp)
         return copy(part_t.at[peer], part_in.at[fsdp], part_ss.at[r], part_rs.at[fsdp], (ctx, peer, batch))
@@ -147,7 +167,7 @@
             rim_copy(r).start()
         vrim_copy().start()
 
-    cols = grad_w.shape[1]
+    cols = tokens.shape[1] // group
 
     def x_copy(r):
         peer = lax.rem(me + r, group)
@@ -157,9 +177,22 @@
             (peer // n_batch, fsdp, lax.rem(peer, n_batch)),
         )
 
+    pair = 2 if n_ctx % 2 == 0 else 1
+    chip, core = ctx // pair, lax.rem(ctx, pair)
+    mate = chip * pair + (pair - 1 - core)
+    late = ctx < n_ctx // 2
+
+    def x_start(first):
+        for r in range(1, group):
+            far = lax.rem(me + r, group) // (n_batch * pair) != chip
+            held = jnp.logical_and(far, late)
+
+            @pl.when(jnp.logical_not(held) if first else held)
+            def _():
+                x_copy(r).start()
+
     if gather:
-        for r in range(1, group):
-            x_copy(r).start()
+        x_start(True)
 
     @pl.when(inner)
     def _():
@@ -179,10 +212,9 @@
     for r in range(1, n_fsdp):
         src = lax.rem(fsdp + r, n_fsdp)
         copy(part_in.at[src], part_in.at[src], part_ss.at[r], part_rs.at[src], (ctx, src, batch)).wait_recv()
-    part_in[fsdp] = part_t[fsdp]
-    raw = part_in[0]
-    for s in range(1, n_fsdp):
-        raw = raw + part_in[s]
+    raw = part_f[fsdp]
+    for r in range(1, n_fsdp):
+        raw = raw + part_in[lax.rem(fsdp + r, n_fsdp)].astype(f32)
     raw = raw.astype(bf16).astype(f32)
 
     @pl.when(inner)
@@ -213,17 +245,69 @@
     q_t = [qk_t[h * 2 * F : h * 2 * F + F] for h in range(heads)]
     k_t = [qk_t[h * 2 * F + F : (h + 1) * 2 * F] for h in range(heads)]
     fk_t = [features(k) for k in k_t]
+
+    def sent(out, into, ss, rs, h, to, i):
+        return copy(out.at[h], into.at[ctx, h], ss.at[i, h], rs.at[ctx, h], (to, fsdp, batch))
+
+    def send(out, into, ss, rs, h, sign, done):
+        def act(c):
+            c.wait_send() if done else c.start()
+
+        if pair == 2:
+            @pl.when(core == (0 if sign > 0 else 1))
+            def _():
+                act(sent(out, into, ss, rs, h, mate, 0))
+
+        for i in range(1, n_ctx // pair):
+            to = ctx + sign * pair * i
+
+            @pl.when(jnp.logical_and(to >= 0, to < n_ctx))
+            def _():
+                act(sent(out, into, ss, rs, h, to, i))
+
+    def passed(into, rs, ps, s, h):
+        return copy(into.at[s, h], into.at[s, h], ps.at[s, h], rs.at[s, h], (mate, fsdp, batch))
+
+    def relays(s, sign):
+        if pair == 1:
+            return s < 0
+        there = s // pair < chip if sign > 0 else s // pair > chip
+        return jnp.logical_and(there, core == s % pair)
+
+    def receive(into, rs, ps, total, h, sign):
+        for s in range(n_ctx):
+            if pair == 2:
+                @pl.when(relays(s, sign))
+                def _():
+                    passed(into, rs, ps, s, h).wait_recv()
+                    passed(into, rs, ps, s, h).start()
+        total[h] = jnp.zeros(total.shape[1:], f32)
+        for s in range(n_ctx):
+            wanted = s < ctx if sign > 0 else s > ctx
+            plain = jnp.logical_and(wanted, jnp.logical_not(relays(s, sign))) if pair == 2 else wanted
+
+            @pl.when(plain)
+            def _():
+                passed(into, rs, ps, s, h).wait_recv()
+
+            @pl.when(wanted)
+            def _():
+                total[h] += into[s, h].astype(f32)
+
+    def finish(out, into, ss, rs, ps, sign):
+        for h in range(heads):
+            send(out, into, ss, rs, h, sign, True)
+            if pair == 2:
+                for s in range(n_ctx):
+                    @pl.when(relays(s, sign))
+                    def _():
+                        passed(into, rs, ps, s, h).wait_send()
+
     for h in range(heads):
-        value = conv_b[:, h * E : (h + 1) * E]
-        state_out[h] = dot(fk_t[h].astype(bf16), value).astype(bf16)
-
-    def state_copy(r):
-        return copy(state_out, state_in.at[ctx], state_ss.at[r], state_rs.at[ctx], (ctx + r, fsdp, batch))
-
-    for r in range(1, n_ctx):
-        @pl.when(ctx + r < n_ctx)
-        def _():
-            state_copy(r).start()
+        state_out[h] = dot(fk_t[h].astype(bf16), conv_b[:, h * E : (h + 1) * E]).astype(bf16)
+        send(state_out, state_in, state_ss, state_rs, h, 1, False)
+    if gather:
+        x_start(False)
 
     fq_t = [features(q) for q in q_t]
     fq = [x.T.astype(bf16) for x in fq_t]
@@ -242,15 +326,11 @@
             jnp.where(at_row <= at_col, 1.0 + score_t + 0.5 * score_t * score_t, 0.0).astype(bf16)
         )
 
-    prior[...] = jnp.zeros(prior.shape, f32)
-    for s in range(n_ctx - 1):
-        @pl.when(s < ctx)
-        def _():
-            copy(state_in.at[s], state_in.at[s], state_ss.at[s], state_rs.at[s], (s, fsdp, batch)).wait_recv()
-            prior[...] += state_in[s].astype(f32)
-    prior_b = [prior[h].astype(bf16) for h in range(heads)]
+    prior_b = []
     for h in range(heads):
         lanes = slice(h * E, (h + 1) * E)
+        receive(state_in, state_rs, pass_s, prior, h, 1)
+        prior_b.append(prior[h].astype(bf16))
         mixed = local[h] + dot(fq[h], prior_b[h])
         inv = lax.rsqrt(jnp.mean(mixed * mixed, axis=-1, keepdims=True) + eps_norm)
         normed = mixed * inv
@@ -259,14 +339,7 @@
         d_mixed = (inv * (g - normed * jnp.mean(g * normed, axis=-1, keepdims=True))).astype(bf16)
         mixed_b[:, lanes] = d_mixed
         grad_out[h] = dot(fq_t[h].astype(bf16), d_mixed).astype(bf16)
-
-    def grad_copy(r):
-        return copy(grad_out, grad_in.at[ctx], grad_ss.at[r], grad_rs.at[ctx], (ctx - r, fsdp, batch))
-
-    for r in range(1, n_ctx):
-        @pl.when(ctx - r >= 0)
-        def _():
-            grad_copy(r).start()
+        send(grad_out, grad_in, grad_ss, grad_rs, h, -1, False)
 
     d_q, d_k, d_v = [], [], []
     for h in range(heads):
@@ -283,19 +356,12 @@
         d_k.append(dot_nt(q_t[h].astype(bf16), d_score_t))
         d_v.append(dot(kernels_t[h], d_mixed))
 
-    later[...] = jnp.zeros(later.shape, f32)
-    for s in range(1, n_ctx):
-        @pl.when(s > ctx)
-        def _():
-            copy(grad_in.at[s], grad_in.at[s], grad_ss.at[s], grad_rs.at[s], (s, fsdp, batch)).wait_recv()
-            later[...] += grad_in[s].astype(f32)
-    rows = []
+    rows, later_b = [], []
     for h in range(heads):
-        lanes = slice(h * E, (h + 1) * E)
-        later_b = later[h].astype(bf16)
-        back = features_back(k_t[h], dot_nt(later_b, conv_b[:, lanes]))
+        receive(grad_in, grad_rs, back_s, later, h, -1)
+        later_b.append(later[h].astype(bf16))
+        back = features_back(k_t[h], dot_nt(later_b[h], conv_b[:, h * E : (h + 1) * E]))
         rows += [d_q[h], d_k[h] + back]
-        dv_ext[0:positions, lanes] = d_v[h] + dot(fk[h], later_b)
     d_qk_t = jnp.concatenate(rows, axis=0)
     dqk_out[...] = d_qk_t
 
@@ -310,6 +376,12 @@
     @pl.when(inner)
     def _():
         dqk_copy().start()
+
+    for h in range(heads):
+        dv_ext[0:positions, h * E : (h + 1) * E] = d_v[h] + dot(fk[h], later_b[h])
+
+    @pl.when(inner)
+    def _():
         dv_copy().start()
 
     @pl.when(outer)
@@ -380,14 +452,18 @@
         dqk_copy().wait_send()
         dv_copy().wait_send()
 
-    for r in range(1, n_ctx):
-        @pl.when(ctx + r < n_ctx)
-        def _():
-            state_copy(r).wait_send()
-
-        @pl.when(ctx - r >= 0)
-        def _():
-            grad_copy(r).wait_send()
+    finish(state_out, state_in, state_ss, state_rs, pass_s, 1)
+    finish(grad_out, grad_in, grad_ss, grad_rs, back_s, -1)
+
+
+def write(*refs):
+    *blocks, sems = refs
+    n = len(blocks) // 2
+    copies = [pltpu.make_async_copy(blocks[i], blocks[n + i], sems.at[i]) for i in range(n)]
+    for c in copies:
+        c.start()
+    for c in copies:
+        c.wait()
 
 
 def shards(dims, inputs, values, w_qk, conv_qk, conv_v, d_attn):
@@ -405,9 +481,17 @@
     dma = pltpu.SemaphoreType.DMA
     state = (heads, PACKED, E)
     vmem = pl.BlockSpec(memory_space=pltpu.VMEM)
+    hbm = pl.BlockSpec(memory_space=pl.ANY)
     scratch = [
+        pltpu.VMEM(tokens.shape, bf16),
+        pltpu.VMEM((positions, wide), bf16),
+        pltpu.VMEM(w_qk.shape, bf16),
+        pltpu.VMEM(conv_qk.shape, f32),
+        pltpu.VMEM(conv_v.shape, f32),
+        pltpu.VMEM((positions, wide), bf16),
         pltpu.VMEM((n_fsdp, width, positions), f32),
-        pltpu.VMEM((n_fsdp, width, positions), f32),
+        pltpu.VMEM((n_fsdp, width, positions), bf16),
+        pltpu.VMEM((n_fsdp, width, positions), bf16),
         pltpu.VMEM((RIM, w_qk.shape[1]), f32),
         pltpu.VMEM((n_fsdp, RIM, w_qk.shape[1]), f32),
         pltpu.VMEM((w_qk.shape[1], positions), f32),
@@ -427,8 +511,10 @@
         pltpu.VMEM((slots, positions, cols if gather else 128), bf16),
         pltpu.VMEM((slots, width, positions), bf16),
         dma((n_fsdp,)), dma((n_fsdp,)), dma((n_fsdp,)), dma((n_fsdp,)), dma, dma,
-        dma((n_ctx,)), dma((n_ctx,)), dma((n_ctx,)), dma((n_ctx,)), dma, dma, dma, dma,
+        dma((n_ctx, heads)), dma((n_ctx, heads)), dma((n_ctx, heads)), dma((n_ctx, heads)),
+        dma, dma, dma, dma,
         dma((slots,)), dma((slots,)), dma((slots,)), dma((slots,)),
+        dma((6,)), dma((n_ctx, heads)), dma((n_ctx, heads)),
     ]
     attended, grad_v, tail = pl.pallas_call(
         functools.partial(body, (n_ctx, n_fsdp, n_batch, gather)),
@@ -437,14 +523,22 @@
             jax.ShapeDtypeStruct((positions, wide), bf16),
             jax.ShapeDtypeStruct(last, f32 if gather else bf16),
         ),
-        in_specs=[vmem] * 6,
+        in_specs=[hbm] * 6,
         out_specs=(vmem,) * 3,
         scratch_shapes=scratch,
         compiler_params=pltpu.CompilerParams(
-            collective_id=0, has_side_effects=True, vmem_limit_bytes=40 * 2**20
+            collective_id=0, has_side_effects=True, vmem_limit_bytes=56 * 2**20
         ),
     )(tokens, values[0], w_qk, conv_qk, conv_v, d_attn[0])
     if gather:
+        blocks = (attended, grad_v, tail)
+        attended, grad_v, tail = pl.pallas_call(
+            write,
+            out_shape=tuple(jax.ShapeDtypeStruct(x.shape, x.dtype) for x in blocks),
+            in_specs=[pl.BlockSpec(memory_space=pltpu.HBM)] * 3,
+            out_specs=(pl.BlockSpec(memory_space=pltpu.HBM),) * 3,
+            scratch_shapes=[dma((3,))],
+        )(*blocks)
         grad_w = tail.T
     else:
         grad_w = lax.psum_scatter(

time: 48.7 us -> 44.7 us (0.918)
  local copies, waits for them, and re-layouts: 7.41 us -> 0 us
  Pallas kernels: 40.3 us -> 44 us
    pallas_call x0 -> x1, Pallas kernels: none -> 13 us  [shards(): pl.pallas_call(write, out_shape=tuple((jax.ShapeDtypeStruct(x.shape, x.dt...]
    pallas_call x1, Pallas kernels: 40.3 us -> 30.9 us  [shards(): pl.pallas_call(functools.partial(body, (n_ctx, n_fsdp, n_batch, gather)),...]
    unnamed x15 -> x0, local copies, waits for them, and re-layouts: 7.41 us -> none
where the time goes in v2:
time: 44.7 us; the launch traced here: 44.6 us
  Pallas kernels  44 us (98%)
  between operations  0.64 us (1%)
    pallas_call x1, Pallas kernels, shards(): pl.pallas_call(functools.partial(body, (n_ctx, n_fsdp, n_batch, gather)),...  30.9 us
    pallas_call x1, Pallas kernels, shards(): pl.pallas_call(write, out_shape=tuple((jax.ShapeDtypeStruct(x.shape, x.dt...  13 us

profile of v2, /device:TPU:0, one launch (start us, length us, event | category | flops | bytes accessed | tf_op | source)
XLA Modules:
  0.0 44.6 jit_solution(11481000729539193297)
XLA Ops:
  0.6 30.9 %shard_map.85 = (bf16[128,512]{1,0:T(8,128)(2,1)}, bf16[128,512]{1,0:T(8,128)(2,1)}, f32[64,512]{1,0:T(8,128)}) custom-call(bf16[128,4096]{1,0:T(8,128)(2,1)} %bitcast.6, bf16[128,512]{1,0:T(8,128)(2,1)} %bitcast.7, bf16[1024,256]{1,0:T(8,128)(2,1)} %weights_h.1, f32[3,64]{1,0:T(4,128)} %conv_qk_h.1, f32[3,512]{1,0:T(4,128)} %conv_v_h.1, ...), custom_call_target="tpu_custom_call" | custom-call | tf_op jit(solution)/shard_map/pallas_call | solution.py:519
  31.6 13.0 %shard_map.86 = (bf16[128,512]{1,0:T(8,128)(2,1)}, bf16[128,512]{1,0:T(8,128)(2,1)}, f32[64,512]{1,0:T(8,128)}) custom-call(bf16[128,512]{1,0:T(8,128)(2,1)} %get-tuple-element.9.refs_0_, bf16[128,512]{1,0:T(8,128)(2,1)} %get-tuple-element.10.refs_1_, f32[64,512]{1,0:T(8,128)} %get-tuple-element.11.refs_2_), custom_call_target="tpu_custom_call" | custom-call | tf_op jit(solution)/shard_map/pallas_call | solution.py:535

commit v3 on v2

--- a/solution.py
+++ b/solution.py
@@ -68,7 +68,7 @@
 def body(
     dims, tokens_h, values_h, weights_h, conv_qk_h, conv_v_h, d_attn_h,
     attended, grad_v, grad_w,
-    tokens, values, weights, conv_qk, conv_v, d_attn,
+    tokens, values, weights, conv_qk, conv_v, d_attn, own,
     part_f, part_t, part_in, rim_out, rim_in, rim_t, vrim_in, ext_v, conv_b,
     state_out, state_in, prior, grad_out, grad_in, later, mixed_b,
     dv_ext, dqk_out, dqk_in, x_in, dq_all,
@@ -121,12 +121,13 @@
         for r in same:
             greet((ctx + 1, lax.rem(fsdp + r, n_fsdp), batch))
 
+    columns = pl.ds(pl.multiple_of(fsdp * depth, depth), depth)
     loads = [
         pltpu.make_async_copy(src, dst, load_s.at[i])
         for i, (src, dst) in enumerate(
             [
-                (weights_h, weights), (tokens_h, tokens), (values_h, values),
-                (conv_v_h, conv_v), (conv_qk_h, conv_qk), (d_attn_h, d_attn),
+                (weights_h, weights), (tokens_h.at[:, columns], own), (values_h, values),
+                (conv_v_h, conv_v), (conv_qk_h, conv_qk), (tokens_h, tokens), (d_attn_h, d_attn),
             ]
         )
     ]
@@ -135,8 +136,7 @@
     loads[0].wait()
     loads[1].wait()
 
-    columns = pl.ds(pl.multiple_of(fsdp * depth, depth), depth)
-    part = dot(tokens[:, columns], weights[...])
+    part = dot(own[...], weights[...])
     part_f[...] = part.T.reshape(part_f.shape)
     part_t[...] = part_f[...].astype(bf16)
     rim_out[...] = part[positions - RIM :]
@@ -192,6 +192,7 @@
                 x_copy(r).start()
 
     if gather:
+        x_in[me] = tokens[:, pl.ds(pl.multiple_of(me * cols, cols), cols)]
         x_start(True)
 
     @pl.when(inner)
@@ -306,9 +307,6 @@
     for h in range(heads):
         state_out[h] = dot(fk_t[h].astype(bf16), conv_b[:, h * E : (h + 1) * E]).astype(bf16)
         send(state_out, state_in, state_ss, state_rs, h, 1, False)
-    if gather:
-        x_start(False)
-
     fq_t = [features(q) for q in q_t]
     fq = [x.T.astype(bf16) for x in fq_t]
     fk = [x.T.astype(bf16) for x in fk_t]
@@ -326,6 +324,9 @@
             jnp.where(at_row <= at_col, 1.0 + score_t + 0.5 * score_t * score_t, 0.0).astype(bf16)
         )
 
+    if gather:
+        x_start(False)
+
     prior_b = []
     for h in range(heads):
         lanes = slice(h * E, (h + 1) * E)
@@ -363,44 +364,6 @@
         back = features_back(k_t[h], dot_nt(later_b[h], conv_b[:, h * E : (h + 1) * E]))
         rows += [d_q[h], d_k[h] + back]
     d_qk_t = jnp.concatenate(rows, axis=0)
-    dqk_out[...] = d_qk_t
-
-    def dv_copy():
-        return copy(
-            dv_ext.at[pl.ds(0, RIM)], dv_ext.at[pl.ds(positions, RIM)], dv_ss, dv_rs, (ctx - 1, fsdp, batch)
-        )
-
-    def dqk_copy():
-        return copy(dqk_out, dqk_in, dqk_ss, dqk_rs, (ctx - 1, fsdp, batch))
-
-    @pl.when(inner)
-    def _():
-        dqk_copy().start()
-
-    for h in range(heads):
-        dv_ext[0:positions, h * E : (h + 1) * E] = d_v[h] + dot(fk[h], later_b[h])
-
-    @pl.when(inner)
-    def _():
-        dv_copy().start()
-
-    @pl.when(outer)
-    def _():
-        dqk_copy().wait_recv()
-
-    @pl.when(jnp.logical_not(outer))
-    def _():
-        dqk_in[...] = jnp.zeros(dqk_in.shape, f32)
-        dv_ext[positions:] = jnp.zeros((RIM, wide), f32)
-
-    after = dqk_in[...]
-    running = taps[0] * d_qk_t
-    for j in range(1, CONV):
-        moved = jnp.where(
-            lane >= positions - j, pltpu.roll(after, positions - j, 1), pltpu.roll(d_qk_t, positions - j, 1)
-        )
-        running = running + taps[j] * moved
-    d_pre = running.astype(bf16)
 
     def dq_copy(r):
         peer = lax.rem(me + r, group)
@@ -409,16 +372,58 @@
             (peer // n_batch, fsdp, lax.rem(peer, n_batch)),
         )
 
+    def dqk_copy():
+        return copy(dqk_out, dqk_in, dqk_ss, dqk_rs, (ctx - 1, fsdp, batch))
+
     if gather:
-        dq_all[me] = d_pre
+        dq_all[me] = d_qk_t.astype(bf16)
         for r in range(1, group):
             dq_copy(r).start()
     else:
-        grad_w[...] = d_pre
+        dqk_out[...] = d_qk_t
+
+        @pl.when(inner)
+        def _():
+            dqk_copy().start()
+
+    def dv_copy():
+        return copy(
+            dv_ext.at[pl.ds(0, RIM)], dv_ext.at[pl.ds(positions, RIM)], dv_ss, dv_rs, (ctx - 1, fsdp, batch)
+        )
+
+    for h in range(heads):
+        dv_ext[0:positions, h * E : (h + 1) * E] = d_v[h] + dot(fk[h], later_b[h])
+
+    @pl.when(inner)
+    def _():
+        dv_copy().start()
+
+    def convolve_back(here, after):
+        running = taps[0] * here
+        for j in range(1, CONV):
+            moved = pltpu.roll(here, positions - j, 1)
+            rim = 0.0 if after is None else pltpu.roll(after, positions - j, 1)
+            running = running + taps[j] * jnp.where(lane >= positions - j, rim, moved)
+        return running.astype(bf16)
+
+    if not gather:
+        @pl.when(outer)
+        def _():
+            dqk_copy().wait_recv()
+
+        @pl.when(jnp.logical_not(outer))
+        def _():
+            dqk_in[...] = jnp.zeros(dqk_in.shape, f32)
+
+        grad_w[...] = convolve_back(d_qk_t, dqk_in[...])
 
     @pl.when(outer)
     def _():
         dv_copy().wait_recv()
+
+    @pl.when(jnp.logical_not(outer))
+    def _():
+        dv_ext[positions:] = jnp.zeros((RIM, wide), f32)
 
     running = conv_v[0:1] * dv_ext[0:positions]
     for j in range(1, CONV):
@@ -426,13 +431,17 @@
     grad_v[...] = running.astype(bf16)
 
     if gather:
-        total = dot(d_pre, tokens[:, pl.ds(pl.multiple_of(me * cols, cols), cols)])
         for r in range(1, group):
             src = lax.rem(me + r, group)
             to = (src // n_batch, fsdp, lax.rem(src, n_batch))
             copy(x_in.at[src], x_in.at[src], x_ss.at[r], x_rs.at[src], to).wait_recv()
             copy(dq_all.at[src], dq_all.at[src], dq_ss.at[r], dq_rs.at[src], to).wait_recv()
-            total = total + dot(dq_all[src], x_in[src])
+        blocks = [dq_all[s].astype(f32) for s in range(group)]
+        d_pre = [
+            convolve_back(blocks[s], blocks[s + n_batch] if s + n_batch < group else None)
+            for s in range(group)
+        ]
+        total = dot(jnp.concatenate(d_pre, axis=1), x_in[...].reshape(group * positions, cols))
         grad_w[...] = total * float(positions * group) ** (-0.5)
         for r in range(1, group):
             x_copy(r).wait_send()
@@ -449,21 +458,12 @@
 
     @pl.when(inner)
     def _():
-        dqk_copy().wait_send()
+        if not gather:
+            dqk_copy().wait_send()
         dv_copy().wait_send()
 
     finish(state_out, state_in, state_ss, state_rs, pass_s, 1)
     finish(grad_out, grad_in, grad_ss, grad_rs, back_s, -1)
-
-
-def write(*refs):
-    *blocks, sems = refs
-    n = len(blocks) // 2
-    copies = [pltpu.make_async_copy(blocks[i], blocks[n + i], sems.at[i]) for i in range(n)]
-    for c in copies:
-        c.start()
-    for c in copies:
-        c.wait()
 
 
 def shards(dims, inputs, values, w_qk, conv_qk, conv_v, d_attn):
@@ -489,6 +489,7 @@
         pltpu.VMEM(conv_qk.shape, f32),
         pltpu.VMEM(conv_v.shape, f32),
         pltpu.VMEM((positions, wide), bf16),
+        pltpu.VMEM((positions, w_qk.shape[0]), bf16),
         pltpu.VMEM((n_fsdp, width, positions), f32),
         pltpu.VMEM((n_fsdp, width, positions), bf16),
         pltpu.VMEM((n_fsdp, width, positions), bf16),
@@ -514,7 +515,7 @@
         dma((n_ctx, heads)), dma((n_ctx, heads)), dma((n_ctx, heads)), dma((n_ctx, heads)),
         dma, dma, dma, dma,
         dma((slots,)), dma((slots,)), dma((slots,)), dma((slots,)),
-        dma((6,)), dma((n_ctx, heads)), dma((n_ctx, heads)),
+        dma((7,)), dma((n_ctx, heads)), dma((n_ctx, heads)),
     ]
     attended, grad_v, tail = pl.pallas_call(
         functools.partial(body, (n_ctx, n_fsdp, n_batch, gather)),
@@ -531,14 +532,6 @@
         ),
     )(tokens, values[0], w_qk, conv_qk, conv_v, d_attn[0])
     if gather:
-        blocks = (attended, grad_v, tail)
-        attended, grad_v, tail = pl.pallas_call(
-            write,
-            out_shape=tuple(jax.ShapeDtypeStruct(x.shape, x.dtype) for x in blocks),
-            in_specs=[pl.BlockSpec(memory_space=pltpu.HBM)] * 3,
-            out_specs=(pl.BlockSpec(memory_space=pltpu.HBM),) * 3,
-            scratch_shapes=[dma((3,))],
-        )(*blocks)
         grad_w = tail.T
     else:
         grad_w = lax.psum_scatter(

time: 44.7 us -> 33.6 us (0.75)
  Pallas kernels: 44 us -> 29.5 us
  local copies, waits for them, and re-layouts: 0 us -> 3.21 us
    pallas_call x1 -> x0, Pallas kernels: 13 us -> none  [shards(): pl.pallas_call(write, out_shape=tuple((jax.ShapeDtypeStruct(x.shape, x.dt...]
    unnamed x0 -> x7, local copies, waits for them, and re-layouts: none -> 3.21 us
    pallas_call x1, Pallas kernels: 30.9 us -> 29.5 us  [shards(): pl.pallas_call(functools.partial(body, (n_ctx, n_fsdp, n_batch, gather)),...]
where the time goes in v3:
time: 33.6 us; the launch traced here: 33.4 us
  Pallas kernels  29.5 us (88%)
  local copies, waits for them, and re-layouts  3.21 us (10%)
  between operations  0.65 us (2%)
    pallas_call x1, Pallas kernels, shards(): pl.pallas_call(functools.partial(body, (n_ctx, n_fsdp, n_batch, gather)),...  29.5 us
    unnamed x7, local copies, waits for them, and re-layouts  3.21 us

profile of v3, /device:TPU:0, one launch (start us, length us, event | category | flops | bytes accessed | tf_op | source)
XLA Modules:
  0.0 33.4 jit_solution(16281458941843077941)
XLA Ops:
  0.6 29.5 %shard_map.85 = (bf16[128,512]{1,0:T(8,128)(2,1)}, bf16[128,512]{1,0:T(8,128)(2,1)}, f32[64,512]{1,0:T(8,128)}) custom-call(bf16[128,4096]{1,0:T(8,128)(2,1)} %bitcast.6, bf16[128,512]{1,0:T(8,128)(2,1)} %bitcast.7, bf16[1024,256]{1,0:T(8,128)(2,1)} %weights_h.1, f32[3,64]{1,0:T(4,128)} %conv_qk_h.1, f32[3,512]{1,0:T(4,128)} %conv_v_h.1, ...), custom_call_target="tpu_custom_call" | custom-call | tf_op jit(solution)/shard_map/pallas_call | solution.py:520
  30.2 0.0 copy-start.1
  30.2 1.6 %copy.12 = bf16[1,128,512]{2,1,0:T(8,128)(2,1)} copy(bf16[1,128,512]{2,1,0:T(8,128)(2,1)} %bitcast.11) | data formatting | bytes 262144
  31.8 0.0 copy-done.1
  31.8 0.0 copy-start
  31.8 0.7 %copy.13 = bf16[1,128,512]{2,1,0:T(8,128)(2,1)} copy(bf16[1,128,512]{2,1,0:T(8,128)(2,1)S(1)} %bitcast.10) | data formatting | bytes 262144
  32.5 0.3 copy-done
  32.8 0.7 %copy.14 = f32[512,64]{0,1:T(8,128)} copy(f32[512,64]{0,1:T(8,128)S(1)} %bitcast.9) | data formatting | bytes 262144
Async XLA Ops:
  30.2 1.6 %copy-start.1 = (bf16[128,512]{1,0:T(8,128)(2,1)S(1)}, bf16[128,512]{1,0:T(8,128)(2,1)}, u32[]{:S(2)}) copy-start(bf16[128,512]{1,0:T(8,128)(2,1)} %get-tuple-element.7) | copy-start | bytes 393220
  31.8 1.0 %copy-start = (f32[64,512]{1,0:T(8,128)S(1)}, f32[64,512]{1,0:T(8,128)}, u32[]{:S(2)}) copy-start(f32[64,512]{1,0:T(8,128)} %get-tuple-element.8) | copy-start | bytes 393220

commit v4 on v3

--- a/solution.py
+++ b/solution.py
@@ -464,6 +464,16 @@
 
     finish(state_out, state_in, state_ss, state_rs, pass_s, 1)
     finish(grad_out, grad_in, grad_ss, grad_rs, back_s, -1)
+
+
+def write(*refs):
+    *blocks, sems = refs
+    n = len(blocks) // 2
+    copies = [pltpu.make_async_copy(blocks[i], blocks[n + i], sems.at[i]) for i in range(n)]
+    for c in copies:
+        c.start()
+    for c in copies:
+        c.wait()
 
 
 def shards(dims, inputs, values, w_qk, conv_qk, conv_v, d_attn):
@@ -517,12 +527,13 @@
         dma((slots,)), dma((slots,)), dma((slots,)), dma((slots,)),
         dma((7,)), dma((n_ctx, heads)), dma((n_ctx, heads)),
     ]
+    place = pltpu.VMEM if gather else jax.ShapeDtypeStruct
     attended, grad_v, tail = pl.pallas_call(
         functools.partial(body, (n_ctx, n_fsdp, n_batch, gather)),
         out_shape=(
-            jax.ShapeDtypeStruct((positions, wide), bf16),
-            jax.ShapeDtypeStruct((positions, wide), bf16),
-            jax.ShapeDtypeStruct(last, f32 if gather else bf16),
+            place((positions, wide), bf16),
+            place((positions, wide), bf16),
+            place(last, f32 if gather else bf16),
         ),
         in_specs=[hbm] * 6,
         out_specs=(vmem,) * 3,
@@ -532,6 +543,14 @@
         ),
     )(tokens, values[0], w_qk, conv_qk, conv_v, d_attn[0])
     if gather:
+        blocks = (attended, grad_v, tail)
+        attended, grad_v, tail = pl.pallas_call(
+            write,
+            out_shape=tuple(jax.ShapeDtypeStruct(x.shape, x.dtype) for x in blocks),
+            in_specs=[vmem] * 3,
+            out_specs=(hbm,) * 3,
+            scratch_shapes=[dma((3,))],
+        )(*blocks)
         grad_w = tail.T
     else:
         grad_w = lax.psum_scatter(

time: 33.6 us -> 33.3 us (level)
  local copies, waits for them, and re-layouts: 3.21 us -> 1.94 us
  Pallas kernels: 29.5 us -> 30.6 us
    pallas_call x0 -> x1, Pallas kernels: none -> 1.79 us  [shards(): pl.pallas_call(write, out_shape=tuple((jax.ShapeDtypeStruct(x.shape, x.dt...]
    unnamed x7 -> x6, local copies, waits for them, and re-layouts: 3.21 us -> 1.94 us
    pallas_call x1, Pallas kernels: 29.5 us -> 28.8 us  [shards(): pl.pallas_call(functools.partial(body, (n_ctx, n_fsdp, n_batch, gather)),...]
where the time goes in v4:
time: 33.3 us; the launch traced here: 33.2 us
  Pallas kernels  30.6 us (92%)
  local copies, waits for them, and re-layouts  1.94 us (6%)
  between operations  0.65 us (2%)
    pallas_call x1, Pallas kernels, shards(): pl.pallas_call(functools.partial(body, (n_ctx, n_fsdp, n_batch, gather)),...  28.8 us
    unnamed x6, local copies, waits for them, and re-layouts  1.94 us
    pallas_call x1, Pallas kernels, shards(): pl.pallas_call(write, out_shape=tuple((jax.ShapeDtypeStruct(x.shape, x.dt...  1.79 us

profile of v4, /device:TPU:0, one launch (start us, length us, event | category | flops | bytes accessed | tf_op | source)
XLA Modules:
  0.0 33.2 jit_solution(1254340639952303388)
XLA Ops:
  0.6 28.8 %shard_map.85 = (bf16[128,512]{1,0:T(8,128)(2,1)S(1)}, bf16[128,512]{1,0:T(8,128)(2,1)S(1)}, f32[64,512]{1,0:T(8,128)S(1)}) custom-call(bf16[128,4096]{1,0:T(8,128)(2,1)} %bitcast.6, bf16[128,512]{1,0:T(8,128)(2,1)} %bitcast.7, bf16[1024,256]{1,0:T(8,128)(2,1)} %weights_h.1, f32[3,64]{1,0:T(4,128)} %conv_qk_h.1, f32[3,512]{1,0:T(4,128)} %conv_v_h.1, ...), custom_call_target="tpu_custom_call" | custom-call | tf_op jit(solution)/shard_map/pallas_call | solution.py:531
  29.4 0.0 copy-start
  29.4 0.6 %copy-done = bf16[128,512]{1,0:T(8,128)(2,1)} copy-done((bf16[128,512]{1,0:T(8,128)(2,1)}, bf16[128,512]{1,0:T(8,128)(2,1)S(1)}, u32[]{:S(2)}) %copy-start) | copy-done | bytes 131096
  30.1 0.0 copy-start.1
  30.1 0.6 %copy-done.1 = bf16[128,512]{1,0:T(8,128)(2,1)} copy-done((bf16[128,512]{1,0:T(8,128)(2,1)}, bf16[128,512]{1,0:T(8,128)(2,1)S(1)}, u32[]{:S(2)}) %copy-start.1) | copy-done | bytes 131096
  30.7 0.0 copy-start.2
  30.7 0.6 %copy-done.2 = f32[64,512]{1,0:T(8,128)} copy-done((f32[64,512]{1,0:T(8,128)}, f32[64,512]{1,0:T(8,128)S(1)}, u32[]{:S(2)}) %copy-start.2) | copy-done | bytes 131096
  31.4 1.8 %shard_map.86 = (bf16[128,512]{1,0:T(8,128)(2,1)}, bf16[128,512]{1,0:T(8,128)(2,1)}, f32[64,512]{1,0:T(8,128)}) custom-call(bf16[128,512]{1,0:T(8,128)(2,1)} %copy-done, bf16[128,512]{1,0:T(8,128)(2,1)} %copy-done.1, f32[64,512]{1,0:T(8,128)} %copy-done.2), custom_call_target="tpu_custom_call" | custom-call | tf_op jit(solution)/shard_map/pallas_call | solution.py:547
Async XLA Ops:
  29.4 0.7 %copy-start = (bf16[128,512]{1,0:T(8,128)(2,1)}, bf16[128,512]{1,0:T(8,128)(2,1)S(1)}, u32[]{:S(2)}) copy-start(bf16[128,512]{1,0:T(8,128)(2,1)S(1)} %get-tuple-element.9.refs_0_) | copy-start | bytes 393220
  30.1 0.6 %copy-start.1 = (bf16[128,512]{1,0:T(8,128)(2,1)}, bf16[128,512]{1,0:T(8,128)(2,1)S(1)}, u32[]{:S(2)}) copy-start(bf16[128,512]{1,0:T(8,128)(2,1)S(1)} %get-tuple-element.10.refs_1_) | copy-start | bytes 393220
  30.7 0.6 %copy-start.2 = (f32[64,512]{1,0:T(8,128)}, f32[64,512]{1,0:T(8,128)S(1)}, u32[]{:S(2)}) copy-start(f32[64,512]{1,0:T(8,128)S(1)} %get-tuple-element.11.refs_2_) | copy-start | bytes 393220

commit v5 on v3

--- a/solution.py
+++ b/solution.py
@@ -71,10 +71,10 @@
     tokens, values, weights, conv_qk, conv_v, d_attn, own,
     part_f, part_t, part_in, rim_out, rim_in, rim_t, vrim_in, ext_v, conv_b,
     state_out, state_in, prior, grad_out, grad_in, later, mixed_b,
-    dv_ext, dqk_out, dqk_in, x_in, dq_all,
+    dv_ext, dqk_out, dqk_in, x_in, dq_all, v_in, k_out, k_in, mixed_f, pulled,
     part_ss, part_rs, rim_ss, rim_rs, vrim_ss, vrim_rs, state_ss, state_rs,
     grad_ss, grad_rs, dv_ss, dv_rs, dqk_ss, dqk_rs, x_ss, x_rs, dq_ss, dq_rs,
-    load_s, pass_s, back_s,
+    load_s, pass_s, back_s, v_ss, v_rs, v_ps, k_ss, k_rs,
 ):
     n_ctx, n_fsdp, n_batch, gather = dims
     ctx, fsdp, batch = lax.axis_index("ctx"), lax.axis_index("fsdp"), lax.axis_index("batch")
@@ -195,60 +195,8 @@
         x_in[me] = tokens[:, pl.ds(pl.multiple_of(me * cols, cols), cols)]
         x_start(True)
 
-    @pl.when(inner)
-    def _():
-        vrim_copy().wait_recv()
-        ext_v[0:RIM_V] = vrim_in[...].astype(f32)
-
-    @pl.when(jnp.logical_not(inner))
-    def _():
-        ext_v[0:RIM_V] = jnp.zeros((RIM_V, wide), f32)
-
-    ext_v[RIM_V:] = values[...].astype(f32)
-    running = conv_v[0:1] * ext_v[RIM_V:]
-    for j in range(1, CONV):
-        running = running + conv_v[j : j + 1] * ext_v[RIM_V - j : RIM_V - j + positions]
-    conv_b[...] = running.astype(bf16)
-
-    for r in range(1, n_fsdp):
-        src = lax.rem(fsdp + r, n_fsdp)
-        copy(part_in.at[src], part_in.at[src], part_ss.at[r], part_rs.at[src], (ctx, src, batch)).wait_recv()
-    raw = part_f[fsdp]
-    for r in range(1, n_fsdp):
-        raw = raw + part_in[lax.rem(fsdp + r, n_fsdp)].astype(f32)
-    raw = raw.astype(bf16).astype(f32)
-
-    @pl.when(inner)
-    def _():
-        for s in range(n_fsdp):
-            copy(rim_in.at[s], rim_in.at[s], rim_ss.at[s], rim_rs.at[s], (ctx - 1, s, batch)).wait_recv()
-        rows = rim_in[0]
-        for s in range(1, n_fsdp):
-            rows = rows + rim_in[s]
-        rows = rows.astype(bf16).astype(f32)
-        block = jnp.concatenate([jnp.zeros((positions - RIM, rows.shape[1]), f32), rows], axis=0)
-        rim_t[...] = block.T
-
-    @pl.when(jnp.logical_not(inner))
-    def _():
-        rim_t[...] = jnp.zeros(rim_t.shape, f32)
-
-    before = rim_t[pl.ds(pl.multiple_of(fsdp * width, width), width), :]
-    lane = lax.broadcasted_iota(jnp.int32, (width, positions), 1)
-    taps = [column_of(conv_qk[j : j + 1]) for j in range(CONV)]
-    running = taps[0] * raw
-    for j in range(1, CONV):
-        moved = jnp.where(lane < j, pltpu.roll(before, j, 1), pltpu.roll(raw, j, 1))
-        running = running + taps[j] * moved
-    qk_t = running.astype(bf16).astype(f32)
-    qk = qk_t.T.astype(bf16)
-
-    q_t = [qk_t[h * 2 * F : h * 2 * F + F] for h in range(heads)]
-    k_t = [qk_t[h * 2 * F + F : (h + 1) * 2 * F] for h in range(heads)]
-    fk_t = [features(k) for k in k_t]
-
     def sent(out, into, ss, rs, h, to, i):
-        return copy(out.at[h], into.at[ctx, h], ss.at[i, h], rs.at[ctx, h], (to, fsdp, batch))
+        return copy(out if out is conv_b else out.at[h], into.at[ctx, h], ss.at[i, h], rs.at[ctx, h], (to, fsdp, batch))
 
     def send(out, into, ss, rs, h, sign, done):
         def act(c):
@@ -296,7 +244,7 @@
                 total[h] += into[s, h].astype(f32)
 
     def finish(out, into, ss, rs, ps, sign):
-        for h in range(heads):
+        for h in range(into.shape[1]):
             send(out, into, ss, rs, h, sign, True)
             if pair == 2:
                 for s in range(n_ctx):
@@ -304,11 +252,80 @@
                     def _():
                         passed(into, rs, ps, s, h).wait_send()
 
-    for h in range(heads):
+    @pl.when(inner)
+    def _():
+        vrim_copy().wait_recv()
+        ext_v[0:RIM_V] = vrim_in[...].astype(f32)
+
+    @pl.when(jnp.logical_not(inner))
+    def _():
+        ext_v[0:RIM_V] = jnp.zeros((RIM_V, wide), f32)
+
+    ext_v[RIM_V:] = values[...].astype(f32)
+    running = conv_v[0:1] * ext_v[RIM_V:]
+    for j in range(1, CONV):
+        running = running + conv_v[j : j + 1] * ext_v[RIM_V - j : RIM_V - j + positions]
+    conv_b[...] = running.astype(bf16)
+    if gather:
+        send(conv_b, v_in, v_ss, v_rs, 0, 1, False)
+
+    for r in range(1, n_fsdp):
+        src = lax.rem(fsdp + r, n_fsdp)
+        copy(part_in.at[src], part_in.at[src], part_ss.at[r], part_rs.at[src], (ctx, src, batch)).wait_recv()
+    raw = part_f[fsdp]
+    for r in range(1, n_fsdp):
+        raw = raw + part_in[lax.rem(fsdp + r, n_fsdp)].astype(f32)
+    raw = raw.astype(bf16).astype(f32)
+
+    @pl.when(inner)
+    def _():
+        for s in range(n_fsdp):
+            copy(rim_in.at[s], rim_in.at[s], rim_ss.at[s], rim_rs.at[s], (ctx - 1, s, batch)).wait_recv()
+        rows = rim_in[0]
+        for s in range(1, n_fsdp):
+            rows = rows + rim_in[s]
+        rows = rows.astype(bf16).astype(f32)
+        block = jnp.concatenate([jnp.zeros((positions - RIM, rows.shape[1]), f32), rows], axis=0)
+        rim_t[...] = block.T
+
+    @pl.when(jnp.logical_not(inner))
+    def _():
+        rim_t[...] = jnp.zeros(rim_t.shape, f32)
+
+    before = rim_t[pl.ds(pl.multiple_of(fsdp * width, width), width), :]
+    lane = lax.broadcasted_iota(jnp.int32, (width, positions), 1)
+    taps = [column_of(conv_qk[j : j + 1]) for j in range(CONV)]
+    running = taps[0] * raw
+    for j in range(1, CONV):
+        moved = jnp.where(lane < j, pltpu.roll(before, j, 1), pltpu.roll(raw, j, 1))
+        running = running + taps[j] * moved
+    qk_t = running.astype(bf16).astype(f32)
+    qk = qk_t.T.astype(bf16)
+
+    q_t = [qk_t[h * 2 * F : h * 2 * F + F] for h in range(heads)]
+    k_t = [qk_t[h * 2 * F + F : (h + 1) * 2 * F] for h in range(heads)]
+    fk_t = [features(k) for k in k_t]
+
+    def k_copy(r):
+        return copy(k_out, k_in.at[ctx], k_ss.at[r], k_rs.at[ctx], (ctx + r, fsdp, batch))
+
+    if gather:
+        k_out[...] = qk_t.astype(bf16)
+        for r in range(1, n_ctx):
+            @pl.when(ctx + r < n_ctx)
+            def _():
+                k_copy(r).start()
+        x_start(False)
+        for i in range(n_ctx):
+            if pair == 2:
+                @pl.when(relays(i, 1))
+                def _():
+                    passed(v_in, v_rs, v_ps, i, 0).wait_recv()
+                    passed(v_in, v_rs, v_ps, i, 0).start()
+    for h in range(0 if gather else heads):
         state_out[h] = dot(fk_t[h].astype(bf16), conv_b[:, h * E : (h + 1) * E]).astype(bf16)
         send(state_out, state_in, state_ss, state_rs, h, 1, False)
     fq_t = [features(q) for q in q_t]
-    fq = [x.T.astype(bf16) for x in fq_t]
     fk = [x.T.astype(bf16) for x in fk_t]
     at_row = lax.broadcasted_iota(jnp.int32, (positions, positions), 0)
     at_col = lax.broadcasted_iota(jnp.int32, (positions, positions), 1)
@@ -324,15 +341,46 @@
             jnp.where(at_row <= at_col, 1.0 + score_t + 0.5 * score_t * score_t, 0.0).astype(bf16)
         )
 
-    if gather:
-        x_start(False)
+    def earlier(act):
+        for i in range(n_ctx - 1):
+            @pl.when(i < ctx)
+            def _():
+                for h in range(heads):
+                    q = qk[:, h * 2 * F : h * 2 * F + F]
+                    k = k_in[i, h * 2 * F + F : (h + 1) * 2 * F]
+                    act(i, h, k, dot(q, k) * F ** (-0.5), v_in[i, 0, :, h * E : (h + 1) * E])
+
+    def mix(i, h, k, score, value):
+        kernel = (1.0 + score + 0.5 * score * score).astype(bf16)
+        mixed_f[:, h * E : (h + 1) * E] += dot(kernel, value)
+
+    def pull(i, h, k, score, value):
+        d_kernel = dot_nt(mixed_b[:, h * E : (h + 1) * E], value)
+        d_score = (d_kernel * (1.0 + score) * F ** (-0.5)).astype(bf16)
+        pulled[h] += dot_nt(k, d_score)
+
+    if gather:
+        for h in range(heads):
+            mixed_f[:, h * E : (h + 1) * E] = local[h]
+        for i in range(n_ctx - 1):
+            @pl.when(i < ctx)
+            def _():
+                copy(k_in.at[i], k_in.at[i], k_ss.at[i], k_rs.at[i], (i, fsdp, batch)).wait_recv()
+
+            @pl.when(jnp.logical_and(i < ctx, jnp.logical_not(relays(i, 1))) if pair == 2 else i < ctx)
+            def _():
+                passed(v_in, v_rs, v_ps, i, 0).wait_recv()
+        earlier(mix)
 
     prior_b = []
     for h in range(heads):
         lanes = slice(h * E, (h + 1) * E)
-        receive(state_in, state_rs, pass_s, prior, h, 1)
-        prior_b.append(prior[h].astype(bf16))
-        mixed = local[h] + dot(fq[h], prior_b[h])
+        if gather:
+            mixed = mixed_f[:, lanes]
+        else:
+            receive(state_in, state_rs, pass_s, prior, h, 1)
+            prior_b.append(prior[h].astype(bf16))
+            mixed = local[h] + dot(fq_t[h].T.astype(bf16), prior_b[h])
         inv = lax.rsqrt(jnp.mean(mixed * mixed, axis=-1, keepdims=True) + eps_norm)
         normed = mixed * inv
         attended[:, lanes] = normed.astype(bf16)
@@ -343,6 +391,9 @@
         send(grad_out, grad_in, grad_ss, grad_rs, h, -1, False)
 
     d_q, d_k, d_v = [], [], []
+    if gather:
+        pulled[...] = jnp.zeros(pulled.shape, f32)
+        earlier(pull)
     for h in range(heads):
         lanes = slice(h * E, (h + 1) * E)
         d_mixed, value = mixed_b[:, lanes], conv_b[:, lanes]
@@ -352,7 +403,8 @@
         ) * F ** (-0.5)
         d_score_t = d_score_t.astype(bf16)
         d_q.append(
-            dot(k_t[h].astype(bf16), d_score_t) + features_back(q_t[h], dot_nt(prior_b[h], d_mixed))
+            dot(k_t[h].astype(bf16), d_score_t)
+            + (pulled[h] if gather else features_back(q_t[h], dot_nt(prior_b[h], d_mixed)))
         )
         d_k.append(dot_nt(q_t[h].astype(bf16), d_score_t))
         d_v.append(dot(kernels_t[h], d_mixed))
@@ -462,7 +514,14 @@
             dqk_copy().wait_send()
         dv_copy().wait_send()
 
-    finish(state_out, state_in, state_ss, state_rs, pass_s, 1)
+    if gather:
+        finish(conv_b, v_in, v_ss, v_rs, v_ps, 1)
+        for r in range(1, n_ctx):
+            @pl.when(ctx + r < n_ctx)
+            def _():
+                k_copy(r).wait_send()
+    else:
+        finish(state_out, state_in, state_ss, state_rs, pass_s, 1)
     finish(grad_out, grad_in, grad_ss, grad_rs, back_s, -1)
 
 
@@ -511,18 +570,25 @@
         pltpu.VMEM((width, positions), f32),
         pltpu.VMEM((slots, positions, cols if gather else 128), bf16),
         pltpu.VMEM((slots, width, positions), bf16),
+        pltpu.VMEM((n_ctx, 1, positions, wide), bf16),
+        pltpu.VMEM((width, positions), bf16),
+        pltpu.VMEM((n_ctx, width, positions), bf16),
+        pltpu.VMEM((positions, wide), f32),
+        pltpu.VMEM((heads, F, positions), f32),
         dma((n_fsdp,)), dma((n_fsdp,)), dma((n_fsdp,)), dma((n_fsdp,)), dma, dma,
         dma((n_ctx, heads)), dma((n_ctx, heads)), dma((n_ctx, heads)), dma((n_ctx, heads)),
         dma, dma, dma, dma,
         dma((slots,)), dma((slots,)), dma((slots,)), dma((slots,)),
         dma((7,)), dma((n_ctx, heads)), dma((n_ctx, heads)),
+        dma((n_ctx, 1)), dma((n_ctx, 1)), dma((n_ctx, 1)), dma((n_ctx,)), dma((n_ctx,)),
     ]
+    place = pltpu.VMEM if gather else jax.ShapeDtypeStruct
     attended, grad_v, tail = pl.pallas_call(
         functools.partial(body, (n_ctx, n_fsdp, n_batch, gather)),
         out_shape=(
-            jax.ShapeDtypeStruct((positions, wide), bf16),
-            jax.ShapeDtypeStruct((positions, wide), bf16),
-            jax.ShapeDtypeStruct(last, f32 if gather else bf16),
+            place((positions, wide), bf16),
+            place((positions, wide), bf16),
+            place(last, f32 if gather else bf16),
         ),
         in_specs=[hbm] * 6,
         out_specs=(vmem,) * 3,

time: 33.6 us -> 31.7 us (0.943)
  local copies, waits for them, and re-layouts: 3.21 us -> 1.97 us
  Pallas kernels: 29.5 us -> 29 us
    unnamed x7 -> x3, local copies, waits for them, and re-layouts: 3.21 us -> 1.97 us
    pallas_call x1, Pallas kernels: 29.5 us -> 29 us  [shards(): pl.pallas_call(functools.partial(body, (n_ctx, n_fsdp, n_batch, gather)),...]
where the time goes in v5:
time: 31.7 us; the launch traced here: 31.6 us
  Pallas kernels  29 us (91%)
  local copies, waits for them, and re-layouts  1.97 us (6%)
  between operations  0.64 us (2%)
    pallas_call x1, Pallas kernels, shards(): pl.pallas_call(functools.partial(body, (n_ctx, n_fsdp, n_batch, gather)),...  29 us
    unnamed x3, local copies, waits for them, and re-layouts  1.97 us

profile of v5, /device:TPU:0, one launch (start us, length us, event | category | flops | bytes accessed | tf_op | source)
XLA Modules:
  0.0 31.6 jit_solution(11429464248090752825)
XLA Ops:
  0.6 29.0 %shard_map.85 = (bf16[128,512]{1,0:T(8,128)(2,1)S(1)}, bf16[128,512]{1,0:T(8,128)(2,1)S(1)}, f32[64,512]{1,0:T(8,128)S(1)}) custom-call(bf16[128,4096]{1,0:T(8,128)(2,1)} %bitcast.9, bf16[128,512]{1,0:T(8,128)(2,1)} %bitcast.10, bf16[1024,256]{1,0:T(8,128)(2,1)} %weights_h.1, f32[3,64]{1,0:T(4,128)} %conv_qk_h.1, f32[3,512]{1,0:T(4,128)} %conv_v_h.1, ...), custom_call_target="tpu_custom_call" | custom-call | tf_op jit(solution)/shard_map/pallas_call | solution.py:586
  29.6 0.7 %copy.12 = bf16[1,128,512]{2,1,0:T(8,128)(2,1)} copy(bf16[1,128,512]{2,1,0:T(8,128)(2,1)S(1)} %bitcast.8) | data formatting | bytes 262144
  30.3 0.7 %copy.13 = bf16[1,128,512]{2,1,0:T(8,128)(2,1)} copy(bf16[1,128,512]{2,1,0:T(8,128)(2,1)S(1)} %bitcast.7) | data formatting | bytes 262144
  30.9 0.7 %copy.14 = f32[512,64]{0,1:T(8,128)} copy(f32[512,64]{0,1:T(8,128)S(1)} %bitcast.6) | data formatting | bytes 262144

commit v6 on v5

--- a/solution.py
+++ b/solution.py
@@ -182,18 +182,20 @@
     mate = chip * pair + (pair - 1 - core)
     late = ctx < n_ctx // 2
 
-    def x_start(first):
+    def x_start(stage):
         for r in range(1, group):
-            far = lax.rem(me + r, group) // (n_batch * pair) != chip
-            held = jnp.logical_and(far, late)
-
-            @pl.when(jnp.logical_not(held) if first else held)
+            peer = lax.rem(me + r, group)
+            far = peer // (n_batch * pair) != chip
+            aside = jnp.logical_and(far, lax.rem(peer, n_batch) != batch)
+            turn = jnp.where(late, jnp.where(far, 1, 0), jnp.where(aside, 2, 0))
+
+            @pl.when(turn == stage)
             def _():
                 x_copy(r).start()
 
     if gather:
         x_in[me] = tokens[:, pl.ds(pl.multiple_of(me * cols, cols), cols)]
-        x_start(True)
+        x_start(0)
 
     def sent(out, into, ss, rs, h, to, i):
         return copy(out if out is conv_b else out.at[h], into.at[ctx, h], ss.at[i, h], rs.at[ctx, h], (to, fsdp, batch))
@@ -315,7 +317,7 @@
             @pl.when(ctx + r < n_ctx)
             def _():
                 k_copy(r).start()
-        x_start(False)
+        x_start(1)
         for i in range(n_ctx):
             if pair == 2:
                 @pl.when(relays(i, 1))
@@ -392,6 +394,7 @@
 
     d_q, d_k, d_v = [], [], []
     if gather:
+        x_start(2)
         pulled[...] = jnp.zeros(pulled.shape, f32)
         earlier(pull)
     for h in range(heads):

time: 31.7 us -> 31.2 us (0.984)
  Pallas kernels: 29 us -> 28.5 us
    pallas_call x1, Pallas kernels: 29 us -> 28.5 us  [shards(): pl.pallas_call(functools.partial(body, (n_ctx, n_fsdp, n_batch, gather)),...]
where the time goes in v6:
time: 31.2 us; the launch traced here: 31.1 us
  Pallas kernels  28.5 us (91%)
  local copies, waits for them, and re-layouts  1.97 us (6%)
  between operations  0.64 us (2%)
    pallas_call x1, Pallas kernels, shards(): pl.pallas_call(functools.partial(body, (n_ctx, n_fsdp, n_batch, gather)),...  28.5 us
    unnamed x3, local copies, waits for them, and re-layouts  1.97 us

profile of v6, /device:TPU:0, one launch (start us, length us, event | category | flops | bytes accessed | tf_op | source)
XLA Modules:
  0.0 31.1 jit_solution(8999115704602833407)
XLA Ops:
  0.6 28.5 %shard_map.85 = (bf16[128,512]{1,0:T(8,128)(2,1)S(1)}, bf16[128,512]{1,0:T(8,128)(2,1)S(1)}, f32[64,512]{1,0:T(8,128)S(1)}) custom-call(bf16[128,4096]{1,0:T(8,128)(2,1)} %bitcast.9, bf16[128,512]{1,0:T(8,128)(2,1)} %bitcast.10, bf16[1024,256]{1,0:T(8,128)(2,1)} %weights_h.1, f32[3,64]{1,0:T(4,128)} %conv_qk_h.1, f32[3,512]{1,0:T(4,128)} %conv_v_h.1, ...), custom_call_target="tpu_custom_call" | custom-call | tf_op jit(solution)/shard_map/pallas_call | solution.py:589
  29.1 0.7 %copy.12 = bf16[1,128,512]{2,1,0:T(8,128)(2,1)} copy(bf16[1,128,512]{2,1,0:T(8,128)(2,1)S(1)} %bitcast.8) | data formatting | bytes 262144
  29.8 0.7 %copy.13 = bf16[1,128,512]{2,1,0:T(8,128)(2,1)} copy(bf16[1,128,512]{2,1,0:T(8,128)(2,1)S(1)} %bitcast.7) | data formatting | bytes 262144
  30.4 0.7 %copy.14 = f32[512,64]{0,1:T(8,128)} copy(f32[512,64]{0,1:T(8,128)S(1)} %bitcast.6) | data formatting | bytes 262144

commit v7 on v6

--- a/solution.py
+++ b/solution.py
@@ -187,7 +187,7 @@
             peer = lax.rem(me + r, group)
             far = peer // (n_batch * pair) != chip
             aside = jnp.logical_and(far, lax.rem(peer, n_batch) != batch)
-            turn = jnp.where(late, jnp.where(far, 1, 0), jnp.where(aside, 2, 0))
+            turn = jnp.where(late, jnp.where(far, 1, 0), jnp.where(aside, 2, jnp.where(far, 1, 0)))
 
             @pl.when(turn == stage)
             def _():
@@ -317,13 +317,13 @@
             @pl.when(ctx + r < n_ctx)
             def _():
                 k_copy(r).start()
-        x_start(1)
         for i in range(n_ctx):
             if pair == 2:
                 @pl.when(relays(i, 1))
                 def _():
                     passed(v_in, v_rs, v_ps, i, 0).wait_recv()
                     passed(v_in, v_rs, v_ps, i, 0).start()
+        x_start(1)
     for h in range(0 if gather else heads):
         state_out[h] = dot(fk_t[h].astype(bf16), conv_b[:, h * E : (h + 1) * E]).astype(bf16)
         send(state_out, state_in, state_ss, state_rs, h, 1, False)

time: 31.2 us -> 34.7 us (1.11)
  Pallas kernels: 28.5 us -> 32 us
    pallas_call x1, Pallas kernels: 28.5 us -> 32 us  [shards(): pl.pallas_call(functools.partial(body, (n_ctx, n_fsdp, n_batch, gather)),...]
where the time goes in v7:
time: 34.7 us; the launch traced here: 34.6 us
  Pallas kernels  32 us (92%)
  local copies, waits for them, and re-layouts  1.97 us (6%)
  between operations  0.64 us (2%)
    pallas_call x1, Pallas kernels, shards(): pl.pallas_call(functools.partial(body, (n_ctx, n_fsdp, n_batch, gather)),...  32 us
    unnamed x3, local copies, waits for them, and re-layouts  1.97 us

profile of v7, /device:TPU:0, one launch (start us, length us, event | category | flops | bytes accessed | tf_op | source)
XLA Modules:
  0.0 34.6 jit_solution(2771785681121032886)
XLA Ops:
  0.6 32.0 %shard_map.85 = (bf16[128,512]{1,0:T(8,128)(2,1)S(1)}, bf16[128,512]{1,0:T(8,128)(2,1)S(1)}, f32[64,512]{1,0:T(8,128)S(1)}) custom-call(bf16[128,4096]{1,0:T(8,128)(2,1)} %bitcast.9, bf16[128,512]{1,0:T(8,128)(2,1)} %bitcast.10, bf16[1024,256]{1,0:T(8,128)(2,1)} %weights_h.1, f32[3,64]{1,0:T(4,128)} %conv_qk_h.1, f32[3,512]{1,0:T(4,128)} %conv_v_h.1, ...), custom_call_target="tpu_custom_call" | custom-call | tf_op jit(solution)/shard_map/pallas_call | solution.py:589
  32.6 0.7 %copy.12 = bf16[1,128,512]{2,1,0:T(8,128)(2,1)} copy(bf16[1,128,512]{2,1,0:T(8,128)(2,1)S(1)} %bitcast.8) | data formatting | bytes 262144
  33.3 0.7 %copy.13 = bf16[1,128,512]{2,1,0:T(8,128)(2,1)} copy(bf16[1,128,512]{2,1,0:T(8,128)(2,1)S(1)} %bitcast.7) | data formatting | bytes 262144
  33.9 0.7 %copy.14 = f32[512,64]{0,1:T(8,128)} copy(f32[512,64]{0,1:T(8,128)S(1)} %bitcast.6) | data formatting | bytes 262144
